TPU v7x, 32 devices: a whole 2x2x4 slice. The times are simulated.
32 devices in a mesh: gx: 4 (over y, core), gy: 4 (over z), sa: 2 (over x).
Axes of the slice: x: 2, y: 2, z: 4, core: 2. Of those that a mesh axis runs over, the one named last changes fastest.
Arguments:
- fields: float32 [2, 7, 16, 32, 512], P('sa', None, 'gx', 'gy'), may hold values from -6 to 6
- sources: float32 [2, 7, 16, 32, 512], P('sa', None, 'gx', 'gy'), may hold values from -5 to 5
- diagonal: float32 [7, 16, 32, 512], P(None, 'gx', 'gy'), may hold values from 0.25 to 2
- block_inverse: float32 [7, 7, 16, 32, 512], P(None, None, 'gx', 'gy'), may hold values from -0.035 to 0.14
- coupling: float32 [7], replicated, may hold values from 0.25 to 0.75
- donors: int32 [16, 3], replicated, may hold values from 0 to 895, as said below
- returns: int32 [4, 896], P('gy'), may hold values from 0 to 15
Outputs:
- fields_out: float32 [2, 7, 16, 32, 512], P('sa', None, 'gx', 'gy')
Inputs may be any that keep to these rules, and one draw needn't show every extreme that they name: `donors`: column 0 is a gy position, column 1 a block index on that position's exit face, column 2 the inflow slot filled; column 2 is a permutation of 0 to 15.
All inputs are finite; a program needn't handle non-finite values.
Results may differ from a plain program's by a relative error of at most 0.00002.
Values sent between devices are 32-bit elements; how exact they have to be, the bound alone decides.
A program may use at most 128 MiB of HBM per device.

v0:
```python
import jax
import jax.numpy as jnp
from jax import lax
from jax.sharding import PartitionSpec as P

SWEEPS = 4
BLK = 32


def swapped(array, axis, apart):
    return lax.ppermute(array, axis, [(i, i ^ 1 << apart) for i in range(lax.axis_size(axis))])


def padded_2(array, sides, width):
    for axis, dim in sides:
        peers, length = (lax.axis_size(axis), array.shape[dim])
        up = [(i, (i + 1) % peers) for i in range(peers - 1)]
        down = [(j, i) for i, j in up]
        last = lax.slice_in_dim(array, length - width, length, axis=dim)
        initial = lax.slice_in_dim(array, 0, width, axis=dim)
        before = lax.ppermute(last, axis, up)
        after = lax.ppermute(initial, axis, down)
        array = jnp.concatenate([before, array, after], axis=dim)
    return array


def z_terms_combustor(values):
    blank_cap = jnp.zeros_like(values[:1, :, :, :1])
    upper_cap = jnp.concatenate([values[1:, :, :, :1], blank_cap], axis=0)
    lower_cap = jnp.concatenate([blank_cap, values[:-1, :, :, -1:]], axis=0)
    upper_terms = jnp.concatenate([values[:, :, :, 1:], upper_cap], axis=3)
    lower_terms = jnp.concatenate([lower_cap, values[:, :, :, :-1]], axis=3)
    return (upper_terms, lower_terms)


def z_terms_turbine(values, inflow):
    upper_cap = jnp.zeros_like(values[:, :, :, :1])
    lower_cap = jnp.concatenate([inflow[None, :, :, None], values[1:, :, :, :1]], axis=0)
    upper_terms = jnp.concatenate([values[:, :, :, 1:], upper_cap], axis=3)
    lower_terms = jnp.concatenate([lower_cap, values[:, :, :, :-1]], axis=3)
    return (upper_terms, lower_terms)


def neighbour_sum(padded, upper_terms, lower_terms):
    summed = padded[:, 2:, 1:-1] + padded[:, :-2, 1:-1]
    summed = summed + padded[:, 1:-1, 2:] + padded[:, 1:-1, :-2]
    return summed + upper_terms + lower_terms


def apply_inverse(block_inverse, driving):
    result = block_inverse[:, 0] * driving[0]
    for column in range(1, driving.shape[0]):
        result = result + block_inverse[:, column] * driving[column]
    return result


def shards(fields, sources, diagonal, block_inverse, coupling, donors, returns):
    values = fields[0]
    source = sources[0]
    state_stack, cells_x, cells_y, cells_z = values.shape
    rows_x = lax.axis_size("gx")
    vertical_rows = lax.axis_size("gy")
    plane_cell_count = rows_x * vertical_rows
    slot_count = cells_x * cells_y // BLK
    face_count = state_stack * cells_y * cells_z // BLK
    slot_total = donors.shape[0]
    section = lax.axis_index("sa")
    place_x = lax.axis_index("gx")
    placement_vertical = lax.axis_index("gy")
    combustor = section == 0
    at_exit = place_x == rows_x - 1
    matches = donors[None, :, 2] == jnp.arange(slot_total, dtype=jnp.int32)[:, None]
    slot_source = jnp.sum(jnp.where(matches, donors[None, :, 0], 0), axis=1)
    slot_block = jnp.sum(jnp.where(matches, donors[None, :, 1], 0), axis=1)
    exit_face = values[:, cells_x - 1].reshape(face_count, BLK)
    sending = combustor & at_exit & (slot_source == placement_vertical)
    downward = jnp.where(sending[:, None], jnp.take(exit_face, slot_block, axis=0), 0.0)
    downward = downward.reshape(plane_cell_count, slot_count, BLK)
    inlet_blocks = values[0, :, :, 0].reshape(slot_count, BLK)
    exit_rows = jnp.arange(plane_cell_count, dtype=jnp.int32) // vertical_rows == rows_x - 1
    upward = jnp.where(
        (exit_rows & jnp.logical_not(combustor))[:, None, None], inlet_blocks[None], 0.0
    )
    outgoing = jnp.stack([upward, downward], axis=1)
    partner_blocks = swapped(outgoing, "sa", 0)
    arrived = lax.all_to_all(partner_blocks, ("gx", "gy"), split_axis=0, concat_axis=0, tiled=True)
    incoming_blocks = arrived[:, ::-1]
    own_index = place_x * vertical_rows + placement_vertical
    own_sources = lax.dynamic_slice_in_dim(slot_source, own_index * slot_count, slot_count)
    inflow_rows = incoming_blocks[
        (rows_x - 1) * vertical_rows + own_sources, 0, jnp.arange(slot_count)
    ]
    inflow = inflow_rows.reshape(cells_x, cells_y)
    wanted = returns[0]
    pressure_back = incoming_blocks[wanted // slot_count, 1, wanted % slot_count].reshape(
        state_stack, cells_y, cells_z
    )
    back_active = combustor & at_exit
    parity = (
        jnp.arange(cells_x)[:, None, None]
        + jnp.arange(cells_y)[None, :, None]
        + jnp.arange(cells_z)[None, None, :]
    ) % 2
    divisor = 6.0 + diagonal
    weights = coupling[:, None, None, None]
    current = values
    for sweep_index in range(SWEEPS):
        for colour in (0, 1):
            padded = padded_2(current, (("gx", 1), ("gy", 2)), 1)
            padded = padded.at[:, -1, 1:-1, :].set(
                jnp.where(back_active, pressure_back, padded[:, -1, 1:-1, :])
            )

            def combustor_step(present):
                upper_terms, lower_terms = z_terms_combustor(present)
                return (source + neighbour_sum(padded, upper_terms, lower_terms)) / divisor

            def turbine_step(present):
                upper_terms, lower_terms = z_terms_turbine(present, inflow)
                driving = source + weights * neighbour_sum(padded, upper_terms, lower_terms)
                return apply_inverse(block_inverse, driving)

            updated = lax.cond(combustor, combustor_step, turbine_step, current)
            current = jnp.where(parity == colour, updated, current)
    return current[None]


def solution(mesh):
    return jax.shard_map(
        shards,
        mesh=mesh,
        in_specs=(
            P("sa", None, "gx", "gy", None),
            P("sa", None, "gx", "gy", None),
            P(None, "gx", "gy", None),
            P(None, None, "gx", "gy", None),
            P(),
            P(),
            P("gy", None),
        ),
        out_specs=P("sa", None, "gx", "gy", None),
        check_vma=False,
    )
```

profile of v0, /device:TPU:6, one launch (start us, length us, event | category | flops | bytes accessed | tf_op | source)
XLA Modules:
  0.0 306.1 jit_solution(2371472283657399535)
XLA Ops:
  4.9 3.4 %collective-permute-start.1 = (f32[7,1,8,512]{3,2,0,1:T(8,128)S(1)}, f32[7,1,8,512]{3,2,0,1:T(8,128)S(1)}, u32[]{:S(2)}, u32[]{:S(2)}) collective-permute-start(f32[7,1,8,512]{3,2,0,1:T(8,128)S(1)} %get-tuple-element.841), channel_id=1, source_target_pairs={{8,0},{16,8},{24,16},{9,1},{17,9},{25,17},{10,2},{18,10},{26,18},{... | collective-permute-start | bytes 344072 | tf_op jit(solution)/shard_map/ppermute | solution.py:22
  10.5 6.4 %all-to-all-start = ((f32[16,2,1,32]{3,2,1,0:T(1,128)}), f32[16,2,1,32]{3,2,1,0:T(1,128)S(1)}, u32[]{:S(2)}, u32[]{:S(2)}) async-start(f32[16,2,1,32]{3,2,1,0:T(1,128)} %copy.643), calls=%async_computation | async-start | bytes 32768 | tf_op jit(solution)/shard_map/all_to_all | solution.py:86
  18.7 3.2 %all-to-all-done = f32[16,2,1,32]{3,2,1,0:T(1,128)S(1)} async-done(((f32[16,2,1,32]{3,2,1,0:T(1,128)}), f32[16,2,1,32]{3,2,1,0:T(1,128)S(1)}, u32[]{:S(2)}, u32[]{:S(2)}) %all-to-all-start) | async-done | bytes 4128 | tf_op jit(solution)/shard_map/all_to_all | solution.py:86
  21.9 5.3 %gather_fusion.1 = f32[896,32]{1,0:T(8,128)S(1)} fusion(f32[16,2,1,32]{3,2,1,0:T(1,128)S(1)} %rev.3, s32[896]{0:T(1024)S(1)} %fusion.176), kind=kCustom, calls=%fused_computation.1 | custom fusion | bytes 240128 | tf_op jit(solution)/shard_map/gather | solution.py:95
  34.0 4.3 %collective-permute-done.3 = f32[7,6,1,512]{3,2,0,1:T(1,128)S(1)} collective-permute-done((f32[7,6,1,512]{3,2,0,1:T(1,128)S(1)}, f32[7,6,1,512]{3,2,0,1:T(1,128)S(1)}, u32[]{:S(2)}, u32[]{:S(2)}) %collective-permute-start.3) | collective-permute-done | bytes 86048 | tf_op jit(solution)/shard_map/ppermute | solution.py:22
  42.2 14.5 %conditional.8 = (f32[7,4,8,512]{3,2,0,1:T(8,128)S(1)}) conditional(s32[]{:T(128)} %convert_element_type.2, (f32[7,7,4,8,512]{4,3,2,1,0:T(8,128)S(1)}, f32[7,1,1,1]{0,3,2,1:T(1,128)}, f32[7,6,10,512]{3,2,0,1:T(8,128)}, f32[7,4,8,512]{3,2,0,1:T(8,128)}, f32[1,32]{1,0:T(1,128)}, /*index=5*/f32[7,4,8,512]{3,2,1,0:T(8,128)}) %tuple.335, ...), branch_computations={%region_2.3_spmd, %region_3.4_spmd} | conditional | flops 2408672 | bytes 12391768 | solution.py:123
  44.6 6.6 %copy.645 = f32[7,4,8,512]{2,1,3,0:T(4,128)} copy(f32[7,4,8,512]{3,2,0,1:T(8,128)} %get-tuple-element.619) | data formatting | bytes 917504 | tf_op jit(solution)/shard_map
  53.3 2.9 fusion.47
  59.8 2.4 collective-permute-start.5
  62.2 3.7 %collective-permute-done.5 = f32[7,1,8,512]{3,2,0,1:T(8,128)S(1)} collective-permute-done((f32[7,1,8,512]{3,2,0,1:T(8,128)S(1)}, f32[7,1,8,512]{3,2,0,1:T(8,128)S(1)}, u32[]{:S(2)}, u32[]{:S(2)}) %collective-permute-start.5) | collective-permute-done | bytes 114720 | tf_op jit(solution)/shard_map/ppermute | solution.py:21
  66.0 2.6 collective-permute-start.7
  70.7 4.3 %collective-permute-done.8 = f32[7,6,1,512]{3,2,0,1:T(1,128)S(1)} collective-permute-done((f32[7,6,1,512]{3,2,0,1:T(1,128)S(1)}, f32[7,6,1,512]{3,2,0,1:T(1,128)S(1)}, u32[]{:S(2)}, u32[]{:S(2)}) %collective-permute-start.8) | collective-permute-done | bytes 86048 | tf_op jit(solution)/shard_map/ppermute | solution.py:22
  78.0 14.5 %conditional.9 = (f32[7,4,8,512]{3,2,0,1:T(8,128)S(1)}) conditional(s32[]{:T(128)} %convert_element_type.2, (f32[7,7,4,8,512]{4,3,2,1,0:T(8,128)S(1)}, f32[7,1,1,1]{0,3,2,1:T(1,128)S(1)}, f32[7,6,10,512]{3,2,0,1:T(8,128)}, f32[7,4,8,512]{3,2,0,1:T(8,128)}, f32[1,32]{1,0:T(1,128)S(1)}, /*index=5*/f32[7,4,8,512]{3,2,1,0:T(8,128)}) %tuple.343, ...), branch_computations={%region_4.5_spmd, %region_5.6_spmd} | conditional | flops 2408672 | bytes 12391088 | solution.py:123
  80.3 6.6 %copy.651 = f32[7,4,8,512]{2,1,3,0:T(4,128)} copy(f32[7,4,8,512]{3,2,0,1:T(8,128)} %get-tuple-element.629) | data formatting | bytes 917504 | tf_op jit(solution)/shard_map
  89.1 2.9 fusion.64
  95.6 2.4 collective-permute-start.9
  98.0 3.7 %collective-permute-done.9 = f32[7,1,8,512]{3,2,0,1:T(8,128)S(1)} collective-permute-done((f32[7,1,8,512]{3,2,0,1:T(8,128)S(1)}, f32[7,1,8,512]{3,2,0,1:T(8,128)S(1)}, u32[]{:S(2)}, u32[]{:S(2)}) %collective-permute-start.9) | collective-permute-done | bytes 114720 | tf_op jit(solution)/shard_map/ppermute | solution.py:21
  101.8 2.5 collective-permute-start.11
  106.4 4.3 %collective-permute-done.12 = f32[7,6,1,512]{3,2,0,1:T(1,128)S(1)} collective-permute-done((f32[7,6,1,512]{3,2,0,1:T(1,128)S(1)}, f32[7,6,1,512]{3,2,0,1:T(1,128)S(1)}, u32[]{:S(2)}, u32[]{:S(2)}) %collective-permute-start.12) | collective-permute-done | bytes 86048 | tf_op jit(solution)/shard_map/ppermute | solution.py:22
  113.7 14.8 %conditional.10 = (f32[7,4,8,512]{3,2,0,1:T(8,128)S(1)}) conditional(s32[]{:T(128)} %convert_element_type.2, (f32[7,7,4,8,512]{4,3,2,1,0:T(8,128)S(1)}, f32[7,1,1,1]{0,3,2,1:T(1,128)S(1)}, f32[7,6,10,512]{3,2,0,1:T(8,128)}, f32[7,4,8,512]{3,2,0,1:T(8,128)}, f32[1,32]{1,0:T(1,128)S(1)}, /*index=5*/f32[7,4,8,512]{3,2,1,0:T(8,128)}) %tuple.344, ...), branch_computations={%region_6.7_spmd, %region_7.8_spmd} | conditional | flops 2408672 | bytes 12391088 | solution.py:123
  116.0 6.6 %copy.657 = f32[7,4,8,512]{2,1,3,0:T(4,128)} copy(f32[7,4,8,512]{3,2,0,1:T(8,128)} %get-tuple-element.639) | data formatting | bytes 917504 | tf_op jit(solution)/shard_map
  124.9 2.9 fusion.81
  134.0 3.7 %collective-permute-done.13 = f32[7,1,8,512]{3,2,0,1:T(8,128)S(1)} collective-permute-done((f32[7,1,8,512]{3,2,0,1:T(8,128)S(1)}, f32[7,1,8,512]{3,2,0,1:T(8,128)S(1)}, u32[]{:S(2)}, u32[]{:S(2)}) %collective-permute-start.13) | collective-permute-done | bytes 114720 | tf_op jit(solution)/shard_map/ppermute | solution.py:21
  141.8 4.3 %collective-permute-done.16 = f32[7,6,1,512]{3,2,0,1:T(1,128)S(1)} collective-permute-done((f32[7,6,1,512]{3,2,0,1:T(1,128)S(1)}, f32[7,6,1,512]{3,2,0,1:T(1,128)S(1)}, u32[]{:S(2)}, u32[]{:S(2)}) %collective-permute-start.16) | collective-permute-done | bytes 86048 | tf_op jit(solution)/shard_map/ppermute | solution.py:22
  149.1 14.6 %conditional.11 = (f32[7,4,8,512]{3,2,0,1:T(8,128)S(1)}) conditional(s32[]{:T(128)} %convert_element_type.2, (f32[7,7,4,8,512]{4,3,2,1,0:T(8,128)S(1)}, f32[7,1,1,1]{0,3,2,1:T(1,128)S(1)}, f32[7,6,10,512]{3,2,0,1:T(8,128)}, f32[7,4,8,512]{3,2,0,1:T(8,128)}, f32[1,32]{1,0:T(1,128)S(1)}, /*index=5*/f32[7,4,8,512]{3,2,1,0:T(8,128)}) %tuple.345, ...), branch_computations={%region_8.9_spmd, %region_9.10_spmd} | conditional | flops 2408672 | bytes 12391088 | solution.py:123
  151.4 6.6 %copy.663 = f32[7,4,8,512]{2,1,3,0:T(4,128)} copy(f32[7,4,8,512]{3,2,0,1:T(8,128)} %get-tuple-element.649) | data formatting | bytes 917504 | tf_op jit(solution)/shard_map
  160.2 2.9 fusion.98
  169.1 3.7 %collective-permute-done.17 = f32[7,1,8,512]{3,2,0,1:T(8,128)S(1)} collective-permute-done((f32[7,1,8,512]{3,2,0,1:T(8,128)S(1)}, f32[7,1,8,512]{3,2,0,1:T(8,128)S(1)}, u32[]{:S(2)}, u32[]{:S(2)}) %collective-permute-start.17) | collective-permute-done | bytes 114720 | tf_op jit(solution)/shard_map/ppermute | solution.py:21
  176.9 4.3 %collective-permute-done.20 = f32[7,6,1,512]{3,2,0,1:T(1,128)S(1)} collective-permute-done((f32[7,6,1,512]{3,2,0,1:T(1,128)S(1)}, f32[7,6,1,512]{3,2,0,1:T(1,128)S(1)}, u32[]{:S(2)}, u32[]{:S(2)}) %collective-permute-start.20) | collective-permute-done | bytes 86048 | tf_op jit(solution)/shard_map/ppermute | solution.py:22
  184.2 14.6 %conditional.12 = (f32[7,4,8,512]{3,2,0,1:T(8,128)S(1)}) conditional(s32[]{:T(128)} %convert_element_type.2, (f32[7,7,4,8,512]{4,3,2,1,0:T(8,128)S(1)}, f32[7,1,1,1]{0,3,2,1:T(1,128)S(1)}, f32[7,6,10,512]{3,2,0,1:T(8,128)}, f32[7,4,8,512]{3,2,0,1:T(8,128)}, f32[1,32]{1,0:T(1,128)S(1)}, /*index=5*/f32[7,4,8,512]{3,2,1,0:T(8,128)}) %tuple.346, ...), branch_computations={%region_10.11_spmd, %region_11.12_spmd} | conditional | flops 2408672 | bytes 12391088 | solution.py:123
  186.5 6.6 %copy.669 = f32[7,4,8,512]{2,1,3,0:T(4,128)} copy(f32[7,4,8,512]{3,2,0,1:T(8,128)} %get-tuple-element.659) | data formatting | bytes 917504 | tf_op jit(solution)/shard_map
  195.4 2.9 fusion.115
  204.3 3.7 %collective-permute-done.21 = f32[7,1,8,512]{3,2,0,1:T(8,128)S(1)} collective-permute-done((f32[7,1,8,512]{3,2,0,1:T(8,128)S(1)}, f32[7,1,8,512]{3,2,0,1:T(8,128)S(1)}, u32[]{:S(2)}, u32[]{:S(2)}) %collective-permute-start.21) | collective-permute-done | bytes 114720 | tf_op jit(solution)/shard_map/ppermute | solution.py:21
  212.1 4.3 %collective-permute-done.24 = f32[7,6,1,512]{3,2,0,1:T(1,128)S(1)} collective-permute-done((f32[7,6,1,512]{3,2,0,1:T(1,128)S(1)}, f32[7,6,1,512]{3,2,0,1:T(1,128)S(1)}, u32[]{:S(2)}, u32[]{:S(2)}) %collective-permute-start.24) | collective-permute-done | bytes 86048 | tf_op jit(solution)/shard_map/ppermute | solution.py:22
  219.4 14.6 %conditional.13 = (f32[7,4,8,512]{3,2,0,1:T(8,128)S(1)}) conditional(s32[]{:T(128)} %convert_element_type.2, (f32[7,7,4,8,512]{4,3,2,1,0:T(8,128)S(1)}, f32[7,1,1,1]{0,3,2,1:T(1,128)S(1)}, f32[7,6,10,512]{3,2,0,1:T(8,128)}, f32[7,4,8,512]{3,2,0,1:T(8,128)}, f32[1,32]{1,0:T(1,128)S(1)}, /*index=5*/f32[7,4,8,512]{3,2,1,0:T(8,128)}) %tuple.347, ...), branch_computations={%region_12.13_spmd, %region_13.14_spmd} | conditional | flops 2408672 | bytes 12391088 | solution.py:123
  221.7 6.6 %copy.675 = f32[7,4,8,512]{2,1,3,0:T(4,128)} copy(f32[7,4,8,512]{3,2,0,1:T(8,128)} %get-tuple-element.669) | data formatting | bytes 917504 | tf_op jit(solution)/shard_map
  230.5 2.9 fusion.132
  237.0 2.4 collective-permute-start.25
  239.4 3.7 %collective-permute-done.25 = f32[7,1,8,512]{3,2,0,1:T(8,128)S(1)} collective-permute-done((f32[7,1,8,512]{3,2,0,1:T(8,128)S(1)}, f32[7,1,8,512]{3,2,0,1:T(8,128)S(1)}, u32[]{:S(2)}, u32[]{:S(2)}) %collective-permute-start.25) | collective-permute-done | bytes 114720 | tf_op jit(solution)/shard_map/ppermute | solution.py:21
  247.2 4.3 %collective-permute-done.28 = f32[7,6,1,512]{3,2,0,1:T(1,128)S(1)} collective-permute-done((f32[7,6,1,512]{3,2,0,1:T(1,128)S(1)}, f32[7,6,1,512]{3,2,0,1:T(1,128)S(1)}, u32[]{:S(2)}, u32[]{:S(2)}) %collective-permute-start.28) | collective-permute-done | bytes 86048 | tf_op jit(solution)/shard_map/ppermute | solution.py:22
  254.5 14.6 %conditional.14 = (f32[7,4,8,512]{3,2,0,1:T(8,128)S(1)}) conditional(s32[]{:T(128)} %convert_element_type.2, (f32[7,7,4,8,512]{4,3,2,1,0:T(8,128)S(1)}, f32[7,1,1,1]{0,3,2,1:T(1,128)S(1)}, f32[7,6,10,512]{3,2,0,1:T(8,128)}, f32[7,4,8,512]{3,2,0,1:T(8,128)}, f32[1,32]{1,0:T(1,128)S(1)}, /*index=5*/f32[7,4,8,512]{3,2,1,0:T(8,128)}) %tuple.348, ...), branch_computations={%region_14.15_spmd, %region_15.16_spmd} | conditional | flops 2408672 | bytes 12391088 | solution.py:123
  256.8 6.6 %copy.681 = f32[7,4,8,512]{2,1,3,0:T(4,128)} copy(f32[7,4,8,512]{3,2,0,1:T(8,128)} %get-tuple-element.679) | data formatting | bytes 917504 | tf_op jit(solution)/shard_map
  265.6 2.9 fusion.149
  274.6 3.7 %collective-permute-done.29 = f32[7,1,8,512]{3,2,0,1:T(8,128)S(1)} collective-permute-done((f32[7,1,8,512]{3,2,0,1:T(8,128)S(1)}, f32[7,1,8,512]{3,2,0,1:T(8,128)S(1)}, u32[]{:S(2)}, u32[]{:S(2)}) %collective-permute-start.29) | collective-permute-done | bytes 114720 | tf_op jit(solution)/shard_map/ppermute | solution.py:21
  282.4 4.3 %collective-permute-done.32 = f32[7,6,1,512]{3,2,0,1:T(1,128)S(1)} collective-permute-done((f32[7,6,1,512]{3,2,0,1:T(1,128)S(1)}, f32[7,6,1,512]{3,2,0,1:T(1,128)S(1)}, u32[]{:S(2)}, u32[]{:S(2)}) %collective-permute-start.32) | collective-permute-done | bytes 86048 | tf_op jit(solution)/shard_map/ppermute | solution.py:22
  289.6 14.6 %conditional.15 = (f32[7,4,8,512]{3,2,0,1:T(8,128)S(1)}) conditional(s32[]{:T(128)} %convert_element_type.2, (f32[7,7,4,8,512]{4,3,2,1,0:T(8,128)S(1)}, f32[7,1,1,1]{0,3,2,1:T(1,128)S(1)}, f32[7,6,10,512]{3,2,0,1:T(8,128)}, f32[7,4,8,512]{3,2,0,1:T(8,128)}, f32[1,32]{1,0:T(1,128)S(1)}, /*index=5*/f32[7,4,8,512]{3,2,1,0:T(8,128)}) %tuple.349, ...), branch_computations={%region_16.17_spmd, %region_17.18_spmd} | conditional | flops 2408672 | bytes 12391088 | solution.py:123
  292.0 6.6 %copy.687 = f32[7,4,8,512]{2,1,3,0:T(4,128)} copy(f32[7,4,8,512]{3,2,0,1:T(8,128)} %get-tuple-element.689) | data formatting | bytes 917504 | tf_op jit(solution)/shard_map
  300.8 2.9 fusion.166
  (237 shorter events, 137.1 us)
Async XLA Ops:
  0.0 16.8 %copy-start.32 = (s32[1,896]{1,0:T(1,128)S(1)}, s32[1,896]{1,0:T(1,128)}, u32[]{:S(2)}) copy-start(s32[1,896]{1,0:T(1,128)} %param.45) | copy-start | bytes 10756
  1.2 26.9 %collective-permute-start = (f32[7,1,8,512]{3,2,0,1:T(8,128)S(1)}, f32[7,1,8,512]{3,2,0,1:T(8,128)S(1)}, u32[]{:S(2)}, u32[]{:S(2)}) collective-permute-start(f32[7,1,8,512]{3,2,0,1:T(8,128)S(1)} %get-tuple-element.840), channel_id=1, source_target_pairs={{0,8},{8,16},{16,24},{1,9},{9,17},{17,25},{2,10},{10,18},{18,26},{... | collective-permute-start | bytes 344072 | tf_op jit(solution)/shard_map/ppermute | solution.py:21
  4.3 5.5 %collective-permute-start.4 = (f32[16,2,1,32]{3,0,2,1:T(8,128)S(1)}, f32[16,2,1,32]{3,0,2,1:T(8,128)S(1)}, u32[]{:S(2)}, u32[]{:S(2)}) collective-permute-start(f32[16,2,1,32]{3,0,2,1:T(8,128)S(1)} %pad_maximum_fusion.40), channel_id=1, source_target_pairs={{0,1},{1,0},{2,3},{3,2},{4,5},{5,4},{6,7},{7,6},{8,9},{9,8},{10,11... | collective-permute-start | bytes 12296 | tf_op jit(solution)/shard_map/ppermute | solution.py:11
  4.9 23.2 %collective-permute-start.1 = (f32[7,1,8,512]{3,2,0,1:T(8,128)S(1)}, f32[7,1,8,512]{3,2,0,1:T(8,128)S(1)}, u32[]{:S(2)}, u32[]{:S(2)}) collective-permute-start(f32[7,1,8,512]{3,2,0,1:T(8,128)S(1)} %get-tuple-element.841), channel_id=1, source_target_pairs={{8,0},{16,8},{24,16},{9,1},{17,9},{25,17},{10,2},{18,10},{26,18},{... | collective-permute-start | bytes 344072 | tf_op jit(solution)/shard_map/ppermute | solution.py:22
  10.5 11.5 %all-to-all-start = ((f32[16,2,1,32]{3,2,1,0:T(1,128)}), f32[16,2,1,32]{3,2,1,0:T(1,128)S(1)}, u32[]{:S(2)}, u32[]{:S(2)}) async-start(f32[16,2,1,32]{3,2,1,0:T(1,128)} %copy.643), calls=%async_computation | async-start | bytes 32768 | tf_op jit(solution)/shard_map/all_to_all | solution.py:86
  27.5 10.9 %copy-start.25 = (f32[1,7,4,8,512]{4,3,1,2,0:T(8,128)S(1)}, f32[1,7,4,8,512]{4,3,1,2,0:T(8,128)}, u32[]{:S(2)}) copy-start(f32[1,7,4,8,512]{4,3,1,2,0:T(8,128)} %copy-done.24) | copy-start | bytes 1376260
  28.1 14.1 %copy-start = (f32[7,7,4,8,512]{4,3,2,1,0:T(8,128)S(1)}, f32[7,7,4,8,512]{4,3,2,1,0:T(8,128)}, u32[]{:S(2)}) copy-start(f32[7,7,4,8,512]{4,3,2,1,0:T(8,128)} %param.42) | copy-start | bytes 9633796
  29.6 4.5 %collective-permute-start.2 = (f32[7,6,1,512]{3,2,0,1:T(1,128)S(1)}, f32[7,6,1,512]{3,2,0,1:T(1,128)S(1)}, u32[]{:S(2)}, u32[]{:S(2)}) collective-permute-start(f32[7,6,1,512]{3,2,0,1:T(1,128)S(1)} %get-tuple-element.824), channel_id=1, source_target_pairs={{0,2},{2,4},{4,6},{1,3},{3,5},{5,7},{8,10},{10,12},{12,14},{9,11},... | collective-permute-start | bytes 258056 | tf_op jit(solution)/shard_map/ppermute | solution.py:21
  32.0 6.4 %collective-permute-start.3 = (f32[7,6,1,512]{3,2,0,1:T(1,128)S(1)}, f32[7,6,1,512]{3,2,0,1:T(1,128)S(1)}, u32[]{:S(2)}, u32[]{:S(2)}) collective-permute-start(f32[7,6,1,512]{3,2,0,1:T(1,128)S(1)} %get-tuple-element.825), channel_id=1, source_target_pairs={{2,0},{4,2},{6,4},{3,1},{5,3},{7,5},{10,8},{12,10},{14,12},{11,9},... | collective-permute-start | bytes 258056 | tf_op jit(solution)/shard_map/ppermute | solution.py:22
  42.2 14.5 %copy-start.29 = (pred[4,8,512]{2,1,0:T(8,128)(4,1)S(1)}, pred[4,8,512]{2,1,0:T(8,128)(4,1)}, u32[]{:S(2)}) copy-start(pred[4,8,512]{2,1,0:T(8,128)(4,1)} %get-tuple-element.843) | copy-start | bytes 49156
  57.9 17.2 %copy-start.11 = (f32[7,4,8,512]{3,2,0,1:T(8,128)}, f32[7,4,8,512]{3,2,0,1:T(8,128)S(1)}, u32[]{:S(2)}) copy-start(f32[7,4,8,512]{3,2,0,1:T(8,128)S(1)} %broadcast_select_fusion.3) | copy-start | bytes 1376260
  57.9 4.3 %collective-permute-start.6 = (f32[7,1,8,512]{3,2,0,1:T(8,128)S(1)}, f32[7,1,8,512]{3,2,0,1:T(8,128)S(1)}, u32[]{:S(2)}, u32[]{:S(2)}) collective-permute-start(f32[7,1,8,512]{3,2,0,1:T(8,128)S(1)} %get-tuple-element.839), channel_id=1, source_target_pairs={{8,0},{16,8},{24,16},{9,1},{17,9},{25,17},{10,2},{18,10},{26,18},{... | collective-permute-start | bytes 344072 | tf_op jit(solution)/shard_map/ppermute | solution.py:22
  59.8 6.1 %collective-permute-start.5 = (f32[7,1,8,512]{3,2,0,1:T(8,128)S(1)}, f32[7,1,8,512]{3,2,0,1:T(8,128)S(1)}, u32[]{:S(2)}, u32[]{:S(2)}) collective-permute-start(f32[7,1,8,512]{3,2,0,1:T(8,128)S(1)} %get-tuple-element.838), channel_id=1, source_target_pairs={{0,8},{8,16},{16,24},{1,9},{9,17},{17,25},{2,10},{10,18},{18,26},{... | collective-permute-start | bytes 344072 | tf_op jit(solution)/shard_map/ppermute | solution.py:21
  66.0 4.6 %collective-permute-start.7 = (f32[7,6,1,512]{3,2,0,1:T(1,128)S(1)}, f32[7,6,1,512]{3,2,0,1:T(1,128)S(1)}, u32[]{:S(2)}, u32[]{:S(2)}) collective-permute-start(f32[7,6,1,512]{3,2,0,1:T(1,128)S(1)} %get-tuple-element.822), channel_id=1, source_target_pairs={{0,2},{2,4},{4,6},{1,3},{3,5},{5,7},{8,10},{10,12},{12,14},{9,11},... | collective-permute-start | bytes 258056 | tf_op jit(solution)/shard_map/ppermute | solution.py:21
  68.6 9.4 %copy-start.30 = (f32[7]{0:T(128)S(1)}, f32[7]{0:T(128)}, u32[]{:S(2)}) copy-start(f32[7]{0:T(128)} %param.43) | copy-start | bytes 88
  68.6 9.4 %copy-start.34 = (f32[1,32]{1,0:T(1,128)S(1)}, f32[1,32]{1,0:T(1,128)}, u32[]{:S(2)}) copy-start(f32[1,32]{1,0:T(1,128)} %dynamic-slice_bitcast_fusion) | copy-start | bytes 388
  68.6 6.4 %collective-permute-start.8 = (f32[7,6,1,512]{3,2,0,1:T(1,128)S(1)}, f32[7,6,1,512]{3,2,0,1:T(1,128)S(1)}, u32[]{:S(2)}, u32[]{:S(2)}) collective-permute-start(f32[7,6,1,512]{3,2,0,1:T(1,128)S(1)} %get-tuple-element.823), channel_id=1, source_target_pairs={{2,0},{4,2},{6,4},{3,1},{5,3},{7,5},{10,8},{12,10},{14,12},{11,9},... | collective-permute-start | bytes 258056 | tf_op jit(solution)/shard_map/ppermute | solution.py:22
  78.0 14.6 %copy-start.28 = (pred[4,8,512]{2,1,0:T(8,128)(4,1)S(1)}, pred[4,8,512]{2,1,0:T(8,128)(4,1)}, u32[]{:S(2)}) copy-start(pred[4,8,512]{2,1,0:T(8,128)(4,1)} %get-tuple-element.842) | copy-start | bytes 49156
  93.7 17.1 %copy-start.12 = (f32[7,4,8,512]{3,2,0,1:T(8,128)}, f32[7,4,8,512]{3,2,0,1:T(8,128)S(1)}, u32[]{:S(2)}) copy-start(f32[7,4,8,512]{3,2,0,1:T(8,128)S(1)} %broadcast_select_fusion.6) | copy-start | bytes 1376260
  93.7 4.3 %collective-permute-start.10 = (f32[7,1,8,512]{3,2,0,1:T(8,128)S(1)}, f32[7,1,8,512]{3,2,0,1:T(8,128)S(1)}, u32[]{:S(2)}, u32[]{:S(2)}) collective-permute-start(f32[7,1,8,512]{3,2,0,1:T(8,128)S(1)} %get-tuple-element.837), channel_id=1, source_target_pairs={{8,0},{16,8},{24,16},{9,1},{17,9},{25,17},{10,2},{18,10},{26,18},{... | collective-permute-start | bytes 344072 | tf_op jit(solution)/shard_map/ppermute | solution.py:22
  95.6 6.1 %collective-permute-start.9 = (f32[7,1,8,512]{3,2,0,1:T(8,128)S(1)}, f32[7,1,8,512]{3,2,0,1:T(8,128)S(1)}, u32[]{:S(2)}, u32[]{:S(2)}) collective-permute-start(f32[7,1,8,512]{3,2,0,1:T(8,128)S(1)} %get-tuple-element.836), channel_id=1, source_target_pairs={{0,8},{8,16},{16,24},{1,9},{9,17},{17,25},{2,10},{10,18},{18,26},{... | collective-permute-start | bytes 344072 | tf_op jit(solution)/shard_map/ppermute | solution.py:21
  101.8 4.6 %collective-permute-start.11 = (f32[7,6,1,512]{3,2,0,1:T(1,128)S(1)}, f32[7,6,1,512]{3,2,0,1:T(1,128)S(1)}, u32[]{:S(2)}, u32[]{:S(2)}) collective-permute-start(f32[7,6,1,512]{3,2,0,1:T(1,128)S(1)} %get-tuple-element.820), channel_id=1, source_target_pairs={{0,2},{2,4},{4,6},{1,3},{3,5},{5,7},{8,10},{10,12},{12,14},{9,11},... | collective-permute-start | bytes 258056 | tf_op jit(solution)/shard_map/ppermute | solution.py:21
  104.4 6.4 %collective-permute-start.12 = (f32[7,6,1,512]{3,2,0,1:T(1,128)S(1)}, f32[7,6,1,512]{3,2,0,1:T(1,128)S(1)}, u32[]{:S(2)}, u32[]{:S(2)}) collective-permute-start(f32[7,6,1,512]{3,2,0,1:T(1,128)S(1)} %get-tuple-element.821), channel_id=1, source_target_pairs={{2,0},{4,2},{6,4},{3,1},{5,3},{7,5},{10,8},{12,10},{14,12},{11,9},... | collective-permute-start | bytes 258056 | tf_op jit(solution)/shard_map/ppermute | solution.py:22
  129.6 16.5 %copy-start.13 = (f32[7,4,8,512]{3,2,0,1:T(8,128)}, f32[7,4,8,512]{3,2,0,1:T(8,128)S(1)}, u32[]{:S(2)}) copy-start(f32[7,4,8,512]{3,2,0,1:T(8,128)S(1)} %broadcast_select_fusion.2) | copy-start | bytes 1376260
  129.6 4.3 %collective-permute-start.14 = (f32[7,1,8,512]{3,2,0,1:T(8,128)S(1)}, f32[7,1,8,512]{3,2,0,1:T(8,128)S(1)}, u32[]{:S(2)}, u32[]{:S(2)}) collective-permute-start(f32[7,1,8,512]{3,2,0,1:T(8,128)S(1)} %get-tuple-element.835), channel_id=1, source_target_pairs={{8,0},{16,8},{24,16},{9,1},{17,9},{25,17},{10,2},{18,10},{26,18},{... | collective-permute-start | bytes 344072 | tf_op jit(solution)/shard_map/ppermute | solution.py:22
  131.6 6.1 %collective-permute-start.13 = (f32[7,1,8,512]{3,2,0,1:T(8,128)S(1)}, f32[7,1,8,512]{3,2,0,1:T(8,128)S(1)}, u32[]{:S(2)}, u32[]{:S(2)}) collective-permute-start(f32[7,1,8,512]{3,2,0,1:T(8,128)S(1)} %get-tuple-element.834), channel_id=1, source_target_pairs={{0,8},{8,16},{16,24},{1,9},{9,17},{17,25},{2,10},{10,18},{18,26},{... | collective-permute-start | bytes 344072 | tf_op jit(solution)/shard_map/ppermute | solution.py:21
  137.8 4.0 %collective-permute-start.15 = (f32[7,6,1,512]{3,2,0,1:T(1,128)S(1)}, f32[7,6,1,512]{3,2,0,1:T(1,128)S(1)}, u32[]{:S(2)}, u32[]{:S(2)}) collective-permute-start(f32[7,6,1,512]{3,2,0,1:T(1,128)S(1)} %get-tuple-element.818), channel_id=1, source_target_pairs={{0,2},{2,4},{4,6},{1,3},{3,5},{5,7},{8,10},{10,12},{12,14},{9,11},... | collective-permute-start | bytes 258056 | tf_op jit(solution)/shard_map/ppermute | solution.py:21
  139.7 6.4 %collective-permute-start.16 = (f32[7,6,1,512]{3,2,0,1:T(1,128)S(1)}, f32[7,6,1,512]{3,2,0,1:T(1,128)S(1)}, u32[]{:S(2)}, u32[]{:S(2)}) collective-permute-start(f32[7,6,1,512]{3,2,0,1:T(1,128)S(1)} %get-tuple-element.819), channel_id=1, source_target_pairs={{2,0},{4,2},{6,4},{3,1},{5,3},{7,5},{10,8},{12,10},{14,12},{11,9},... | collective-permute-start | bytes 258056 | tf_op jit(solution)/shard_map/ppermute | solution.py:22
  164.7 16.5 %copy-start.14 = (f32[7,4,8,512]{3,2,0,1:T(8,128)}, f32[7,4,8,512]{3,2,0,1:T(8,128)S(1)}, u32[]{:S(2)}) copy-start(f32[7,4,8,512]{3,2,0,1:T(8,128)S(1)} %broadcast_select_fusion.5) | copy-start | bytes 1376260
  164.8 4.3 %collective-permute-start.18 = (f32[7,1,8,512]{3,2,0,1:T(8,128)S(1)}, f32[7,1,8,512]{3,2,0,1:T(8,128)S(1)}, u32[]{:S(2)}, u32[]{:S(2)}) collective-permute-start(f32[7,1,8,512]{3,2,0,1:T(8,128)S(1)} %get-tuple-element.833), channel_id=1, source_target_pairs={{8,0},{16,8},{24,16},{9,1},{17,9},{25,17},{10,2},{18,10},{26,18},{... | collective-permute-start | bytes 344072 | tf_op jit(solution)/shard_map/ppermute | solution.py:22
  166.7 6.1 %collective-permute-start.17 = (f32[7,1,8,512]{3,2,0,1:T(8,128)S(1)}, f32[7,1,8,512]{3,2,0,1:T(8,128)S(1)}, u32[]{:S(2)}, u32[]{:S(2)}) collective-permute-start(f32[7,1,8,512]{3,2,0,1:T(8,128)S(1)} %get-tuple-element.832), channel_id=1, source_target_pairs={{0,8},{8,16},{16,24},{1,9},{9,17},{17,25},{2,10},{10,18},{18,26},{... | collective-permute-start | bytes 344072 | tf_op jit(solution)/shard_map/ppermute | solution.py:21
  172.9 4.0 %collective-permute-start.19 = (f32[7,6,1,512]{3,2,0,1:T(1,128)S(1)}, f32[7,6,1,512]{3,2,0,1:T(1,128)S(1)}, u32[]{:S(2)}, u32[]{:S(2)}) collective-permute-start(f32[7,6,1,512]{3,2,0,1:T(1,128)S(1)} %get-tuple-element.816), channel_id=1, source_target_pairs={{0,2},{2,4},{4,6},{1,3},{3,5},{5,7},{8,10},{10,12},{12,14},{9,11},... | collective-permute-start | bytes 258056 | tf_op jit(solution)/shard_map/ppermute | solution.py:21
  174.8 6.4 %collective-permute-start.20 = (f32[7,6,1,512]{3,2,0,1:T(1,128)S(1)}, f32[7,6,1,512]{3,2,0,1:T(1,128)S(1)}, u32[]{:S(2)}, u32[]{:S(2)}) collective-permute-start(f32[7,6,1,512]{3,2,0,1:T(1,128)S(1)} %get-tuple-element.817), channel_id=1, source_target_pairs={{2,0},{4,2},{6,4},{3,1},{5,3},{7,5},{10,8},{12,10},{14,12},{11,9},... | collective-permute-start | bytes 258056 | tf_op jit(solution)/shard_map/ppermute | solution.py:22
  199.9 16.5 %copy-start.15 = (f32[7,4,8,512]{3,2,0,1:T(8,128)}, f32[7,4,8,512]{3,2,0,1:T(8,128)S(1)}, u32[]{:S(2)}) copy-start(f32[7,4,8,512]{3,2,0,1:T(8,128)S(1)} %broadcast_select_fusion.1) | copy-start | bytes 1376260
  199.9 4.3 %collective-permute-start.22 = (f32[7,1,8,512]{3,2,0,1:T(8,128)S(1)}, f32[7,1,8,512]{3,2,0,1:T(8,128)S(1)}, u32[]{:S(2)}, u32[]{:S(2)}) collective-permute-start(f32[7,1,8,512]{3,2,0,1:T(8,128)S(1)} %get-tuple-element.831), channel_id=1, source_target_pairs={{8,0},{16,8},{24,16},{9,1},{17,9},{25,17},{10,2},{18,10},{26,18},{... | collective-permute-start | bytes 344072 | tf_op jit(solution)/shard_map/ppermute | solution.py:22
  201.8 6.1 %collective-permute-start.21 = (f32[7,1,8,512]{3,2,0,1:T(8,128)S(1)}, f32[7,1,8,512]{3,2,0,1:T(8,128)S(1)}, u32[]{:S(2)}, u32[]{:S(2)}) collective-permute-start(f32[7,1,8,512]{3,2,0,1:T(8,128)S(1)} %get-tuple-element.830), channel_id=1, source_target_pairs={{0,8},{8,16},{16,24},{1,9},{9,17},{17,25},{2,10},{10,18},{18,26},{... | collective-permute-start | bytes 344072 | tf_op jit(solution)/shard_map/ppermute | solution.py:21
  208.1 4.0 %collective-permute-start.23 = (f32[7,6,1,512]{3,2,0,1:T(1,128)S(1)}, f32[7,6,1,512]{3,2,0,1:T(1,128)S(1)}, u32[]{:S(2)}, u32[]{:S(2)}) collective-permute-start(f32[7,6,1,512]{3,2,0,1:T(1,128)S(1)} %get-tuple-element.814), channel_id=1, source_target_pairs={{0,2},{2,4},{4,6},{1,3},{3,5},{5,7},{8,10},{10,12},{12,14},{9,11},... | collective-permute-start | bytes 258056 | tf_op jit(solution)/shard_map/ppermute | solution.py:21
  210.0 6.4 %collective-permute-start.24 = (f32[7,6,1,512]{3,2,0,1:T(1,128)S(1)}, f32[7,6,1,512]{3,2,0,1:T(1,128)S(1)}, u32[]{:S(2)}, u32[]{:S(2)}) collective-permute-start(f32[7,6,1,512]{3,2,0,1:T(1,128)S(1)} %get-tuple-element.815), channel_id=1, source_target_pairs={{2,0},{4,2},{6,4},{3,1},{5,3},{7,5},{10,8},{12,10},{14,12},{11,9},... | collective-permute-start | bytes 258056 | tf_op jit(solution)/shard_map/ppermute | solution.py:22
  235.0 16.5 %copy-start.10 = (f32[7,4,8,512]{3,2,0,1:T(8,128)}, f32[7,4,8,512]{3,2,0,1:T(8,128)S(1)}, u32[]{:S(2)}) copy-start(f32[7,4,8,512]{3,2,0,1:T(8,128)S(1)} %broadcast_select_fusion.4) | copy-start | bytes 1376260
  235.1 4.3 %collective-permute-start.26 = (f32[7,1,8,512]{3,2,0,1:T(8,128)S(1)}, f32[7,1,8,512]{3,2,0,1:T(8,128)S(1)}, u32[]{:S(2)}, u32[]{:S(2)}) collective-permute-start(f32[7,1,8,512]{3,2,0,1:T(8,128)S(1)} %get-tuple-element.829), channel_id=1, source_target_pairs={{8,0},{16,8},{24,16},{9,1},{17,9},{25,17},{10,2},{18,10},{26,18},{... | collective-permute-start | bytes 344072 | tf_op jit(solution)/shard_map/ppermute | solution.py:22
  237.0 6.1 %collective-permute-start.25 = (f32[7,1,8,512]{3,2,0,1:T(8,128)S(1)}, f32[7,1,8,512]{3,2,0,1:T(8,128)S(1)}, u32[]{:S(2)}, u32[]{:S(2)}) collective-permute-start(f32[7,1,8,512]{3,2,0,1:T(8,128)S(1)} %get-tuple-element.828), channel_id=1, source_target_pairs={{0,8},{8,16},{16,24},{1,9},{9,17},{17,25},{2,10},{10,18},{18,26},{... | collective-permute-start | bytes 344072 | tf_op jit(solution)/shard_map/ppermute | solution.py:21
  243.2 4.0 %collective-permute-start.27 = (f32[7,6,1,512]{3,2,0,1:T(1,128)S(1)}, f32[7,6,1,512]{3,2,0,1:T(1,128)S(1)}, u32[]{:S(2)}, u32[]{:S(2)}) collective-permute-start(f32[7,6,1,512]{3,2,0,1:T(1,128)S(1)} %get-tuple-element.812), channel_id=1, source_target_pairs={{0,2},{2,4},{4,6},{1,3},{3,5},{5,7},{8,10},{10,12},{12,14},{9,11},... | collective-permute-start | bytes 258056 | tf_op jit(solution)/shard_map/ppermute | solution.py:21
  245.1 6.4 %collective-permute-start.28 = (f32[7,6,1,512]{3,2,0,1:T(1,128)S(1)}, f32[7,6,1,512]{3,2,0,1:T(1,128)S(1)}, u32[]{:S(2)}, u32[]{:S(2)}) collective-permute-start(f32[7,6,1,512]{3,2,0,1:T(1,128)S(1)} %get-tuple-element.813), channel_id=1, source_target_pairs={{2,0},{4,2},{6,4},{3,1},{5,3},{7,5},{10,8},{12,10},{14,12},{11,9},... | collective-permute-start | bytes 258056 | tf_op jit(solution)/shard_map/ppermute | solution.py:22
  270.2 16.5 %copy-start.9 = (f32[7,4,8,512]{3,2,0,1:T(8,128)}, f32[7,4,8,512]{3,2,0,1:T(8,128)S(1)}, u32[]{:S(2)}) copy-start(f32[7,4,8,512]{3,2,0,1:T(8,128)S(1)} %broadcast_select_fusion) | copy-start | bytes 1376260
  270.2 4.3 %collective-permute-start.30 = (f32[7,1,8,512]{3,2,0,1:T(8,128)S(1)}, f32[7,1,8,512]{3,2,0,1:T(8,128)S(1)}, u32[]{:S(2)}, u32[]{:S(2)}) collective-permute-start(f32[7,1,8,512]{3,2,0,1:T(8,128)S(1)} %get-tuple-element.827), channel_id=1, source_target_pairs={{8,0},{16,8},{24,16},{9,1},{17,9},{25,17},{10,2},{18,10},{26,18},{... | collective-permute-start | bytes 344072 | tf_op jit(solution)/shard_map/ppermute | solution.py:22
  272.1 6.1 %collective-permute-start.29 = (f32[7,1,8,512]{3,2,0,1:T(8,128)S(1)}, f32[7,1,8,512]{3,2,0,1:T(8,128)S(1)}, u32[]{:S(2)}, u32[]{:S(2)}) collective-permute-start(f32[7,1,8,512]{3,2,0,1:T(8,128)S(1)} %get-tuple-element.826), channel_id=1, source_target_pairs={{0,8},{8,16},{16,24},{1,9},{9,17},{17,25},{2,10},{10,18},{18,26},{... | collective-permute-start | bytes 344072 | tf_op jit(solution)/shard_map/ppermute | solution.py:21
  278.4 4.0 %collective-permute-start.31 = (f32[7,6,1,512]{3,2,0,1:T(1,128)S(1)}, f32[7,6,1,512]{3,2,0,1:T(1,128)S(1)}, u32[]{:S(2)}, u32[]{:S(2)}) collective-permute-start(f32[7,6,1,512]{3,2,0,1:T(1,128)S(1)} %get-tuple-element.810), channel_id=1, source_target_pairs={{0,2},{2,4},{4,6},{1,3},{3,5},{5,7},{8,10},{10,12},{12,14},{9,11},... | collective-permute-start | bytes 258056 | tf_op jit(solution)/shard_map/ppermute | solution.py:21
  280.3 6.4 %collective-permute-start.32 = (f32[7,6,1,512]{3,2,0,1:T(1,128)S(1)}, f32[7,6,1,512]{3,2,0,1:T(1,128)S(1)}, u32[]{:S(2)}, u32[]{:S(2)}) collective-permute-start(f32[7,6,1,512]{3,2,0,1:T(1,128)S(1)} %get-tuple-element.811), channel_id=1, source_target_pairs={{2,0},{4,2},{6,4},{3,1},{5,3},{7,5},{10,8},{12,10},{14,12},{11,9},... | collective-permute-start | bytes 258056 | tf_op jit(solution)/shard_map/ppermute | solution.py:22
  (6 other events, 41.4 us)
where the time goes:
time: 310 us; the launch traced here: 306 us
  local copies, waits for them, and re-layouts  108 us (35%)
  starting transfers between devices  69.9 us (23%)
  waiting for transfers between devices  69.5 us (22%)
  other arithmetic  56.4 us (18%)
    another operation x16, local copies, waits for them, and re-layouts  57.1 us
    ppermute x16, starting transfers between devices, padded_2(): before = lax.ppermute(last, axis, up)  35.9 us
    ppermute x16, waiting for transfers between devices, padded_2(): after = lax.ppermute(initial, axis, down)  34.5 us
    ppermute x16, waiting for transfers between devices, padded_2(): before = lax.ppermute(last, axis, up)  31.8 us
    ppermute x16, starting transfers between devices, padded_2(): after = lax.ppermute(initial, axis, down)  27.1 us
    add x8, other arithmetic, turbine_step(): driving = source + weights * neighbour_sum(padded, upper_terms, lower_terms)  23.1 us
    slice x8, local copies, waits for them, and re-layouts, z_terms_turbine(): upper_terms = jnp.concatenate([values[:, :, :, 1:], upper_cap], axis=3)  18.6 us
    scatter x8, local copies, waits for them, and re-layouts, shards(): padded.at[:, -1, 1:-1, :]  13.1 us
  transfers between devices with their start and end apart: 34, of which 24 were waited for; matrix products, arithmetic and copies ran while one was open for 3% of the time, Pallas kernels for 0%

commit v1 on v0

v1 whole, which is shorter than its diff:
```python
import functools

import jax
import jax.numpy as jnp
from jax import lax
from jax.experimental import pallas as pl
from jax.experimental.pallas import tpu as pltpu
from jax.sharding import PartitionSpec as P

SWEEPS = 4
BLK = 32
LANES = 128
MESH = pl.DeviceIdType.MESH


def kernel(
    n_gx, n_gy, sizes,
    fields, sources, diagonal, inverse, coupling, donors, returns, out,
    raw, raw_source, raw_diagonal, raw_inverse, held, source, scale, matrix, part,
    halo_x, halo_y, edge_y, inflow, wanted, table, rows, inlet, arrived,
    local_sem, send_sem, recv_sem, slot_sem, interface_sem,
):
    states, cells_x, cells_y, cells_z = sizes
    pairs = cells_x // 2
    halves = 2 * SWEEPS
    slots = n_gx * n_gy
    per_row = cells_z // BLK
    gx, gy, sa = lax.axis_index("gx"), lax.axis_index("gy"), lax.axis_index("sa")
    own = gx * n_gy + gy
    has = (
        (gx + n_gx - 1) // n_gx,
        1 - (gx + 1) // n_gx,
        (gy + n_gy - 1) // n_gy,
        1 - (gy + 1) // n_gy,
    )
    peers = ({"gx": gx - 1}, {"gx": gx + 1}, {"gy": gy - 1}, {"gy": gy + 1})
    combustor = sa == 0
    turbine = sa == 1
    at_exit = combustor & (gx == n_gx - 1)

    load_fields = pltpu.make_async_copy(fields.at[0], raw, local_sem.at[0])
    load_source = pltpu.make_async_copy(sources.at[0], raw_source, local_sem.at[1])
    load_diagonal = pltpu.make_async_copy(diagonal, raw_diagonal, local_sem.at[2])
    load_inverse = pltpu.make_async_copy(inverse, raw_inverse, local_sem.at[3])
    load_fields.start()
    load_source.start()
    pl.when(combustor)(load_diagonal.start)
    pl.when(turbine)(load_inverse.start)

    barrier = pltpu.get_barrier_semaphore()

    def greet(peer):
        pl.semaphore_signal(barrier, inc=1, device_id=peer, device_id_type=MESH)

    for there, peer in zip(has, peers):
        pl.when(there == 1)(functools.partial(greet, peer))

    @pl.when(turbine)
    def _():
        for j in range(n_gy):
            greet({"gx": n_gx - 1, "gy": j, "sa": 0})

    @pl.when(at_exit)
    def _():
        for g in range(slots):
            greet({"gx": g // n_gy, "gy": g % n_gy, "sa": 1})

    sub = lax.broadcasted_iota(jnp.int32, (cells_y, LANES), 0)
    lane = lax.broadcasted_iota(jnp.int32, (cells_y, LANES), 1)
    tall = lax.broadcasted_iota(jnp.int32, (cells_y, cells_z), 0)
    wide = lax.broadcasted_iota(jnp.int32, (cells_y, cells_z), 1)
    parity = (tall + wide) % 2
    even = parity == 0
    even_lanes = (sub + lane) % 2 == 0

    def split(even_plane, odd_plane):
        return (jnp.where(even, even_plane, odd_plane), jnp.where(even, odd_plane, even_plane))

    def stage_y(colour):
        for p in range(pairs):
            for k in range(states):
                edge_y[0, colour, p, k] = held[colour, p, k, 0:1, :]
                edge_y[1, colour, p, k] = held[colour, p, k, cells_y - 1 : cells_y, :]

    def halo_copy(way, colour, half):
        if way == 0:
            ends = (held.at[colour, 0], halo_x.at[1, half])
        elif way == 1:
            ends = (held.at[colour, pairs - 1], halo_x.at[0, half])
        else:
            ends = (edge_y.at[way - 2, colour], halo_y.at[3 - way, half])
        return pltpu.make_async_remote_copy(
            src_ref=ends[0],
            dst_ref=ends[1],
            send_sem=send_sem.at[way, half],
            recv_sem=recv_sem.at[way, half],
            device_id=peers[way],
            device_id_type=MESH,
        )

    def send(ways, colour, half):
        for way in ways:
            pl.when(has[way] == 1)(lambda way=way: halo_copy(way, colour, half).start())

    def wait_sent(colour, half):
        for way in range(4):
            pl.when(has[way] == 1)(lambda way=way: halo_copy(way, colour, half).wait_send())

    def wait_received(colour, half):
        for way in range(4):
            pl.when(has[way] == 1)(lambda way=way: halo_copy(way ^ 1, colour, half).wait_recv())

    def inlet_copy(j):
        return pltpu.make_async_remote_copy(
            src_ref=inlet.at[0],
            dst_ref=table.at[own],
            send_sem=slot_sem.at[j],
            recv_sem=interface_sem.at[0],
            device_id={"gx": n_gx - 1, "gy": j, "sa": 0},
            device_id_type=MESH,
        )

    def row_copy(g):
        return pltpu.make_async_remote_copy(
            src_ref=rows.at[g],
            dst_ref=arrived.at[gy],
            send_sem=slot_sem.at[g],
            recv_sem=interface_sem.at[1],
            device_id={"gx": g // n_gy, "gy": g % n_gy, "sa": 1},
            device_id_type=MESH,
        )

    @pl.when(has[0] == 0)
    def _():
        halo_x[0, 0] = jnp.zeros((states, cells_y, cells_z), jnp.float32)

    @pl.when((has[1] == 0) & turbine)
    def _():
        halo_x[1, 0] = jnp.zeros((states, cells_y, cells_z), jnp.float32)

    for side in range(2):
        @pl.when(has[2 + side] == 0)
        def _():
            halo_y[side, 0] = jnp.zeros((pairs, states, 1, cells_z), jnp.float32)

    load_fields.wait()
    for k in range(states):
        for p in range(pairs):
            held[0, p, k], held[1, p, k] = split(raw[k, 2 * p], raw[k, 2 * p + 1])
    stage_y(1)

    @pl.when(turbine)
    def _():
        row = jnp.zeros((cells_y, LANES), jnp.float32)
        for x in range(cells_x):
            row = jnp.where(lane % BLK == x * cells_y + sub, raw[0, x, :, 0:1], row)
        inlet[0] = jnp.sum(row, axis=0, keepdims=True)

    @pl.when(at_exit)
    def _():
        slot_row = lax.broadcasted_iota(jnp.int32, (slots, LANES), 0)
        in_state = tall * per_row + wide // BLK

        def take(e, total):
            block = jnp.where(donors[e, 0] == gy, donors[e, 1], -1)
            found = jnp.zeros((cells_y, cells_z), jnp.float32)
            for k in range(states):
                here = in_state == block - k * (cells_y * per_row)
                found = jnp.where(here, raw[k, cells_x - 1], found)
            row = jnp.sum(found, axis=0, keepdims=True)
            row = sum(row[:, i * LANES : (i + 1) * LANES] for i in range(cells_z // LANES))
            return jnp.where(slot_row == donors[e, 2], row, total)

        total = lax.fori_loop(0, slots, take, jnp.zeros((slots, LANES), jnp.float32))
        for g in range(slots):
            rows[g] = total[g : g + 1]

    met = has[0] + has[1] + has[2] + has[3] + sa * n_gy + (1 - sa) * (1 - has[1]) * slots
    pl.semaphore_wait(barrier, met)
    send(range(4), 1, 0)

    @pl.when(turbine)
    def _():
        for j in range(n_gy):
            inlet_copy(j).start()

    @pl.when(at_exit)
    def _():
        for g in range(slots):
            row_copy(g).start()

        spread_from = lax.broadcasted_iota(jnp.int32, (LANES, cells_z), 0) % per_row
        spread_to = lax.broadcasted_iota(jnp.int32, (LANES, cells_z), 1) // BLK
        spread = jnp.where(spread_from == spread_to, 1.0, 0.0)
        for k in range(states):
            ids = returns[0:1, k * LANES : (k + 1) * LANES].astype(jnp.float32)
            ids = jnp.where(lane // per_row == sub, ids, 0.0)
            wanted[k] = jnp.dot(
                ids, spread, precision=lax.Precision.HIGHEST, preferred_element_type=jnp.float32
            )

    load_source.wait()
    for k in range(states):
        for p in range(pairs):
            source[0, p, k], source[1, p, k] = split(raw_source[k, 2 * p], raw_source[k, 2 * p + 1])

    @pl.when(combustor)
    def _():
        load_diagonal.wait()
        for k in range(states):
            for p in range(pairs):
                first, second = split(raw_diagonal[k, 2 * p], raw_diagonal[k, 2 * p + 1])
                scale[0, p, k] = 1.0 / (6.0 + first)
                scale[1, p, k] = 1.0 / (6.0 + second)

    @pl.when(turbine)
    def _():
        load_inverse.wait()

        def pack(s, carry):
            for t in range(states):
                for p in range(pairs):
                    first, second = split(raw_inverse[s, t, 2 * p], raw_inverse[s, t, 2 * p + 1])
                    matrix[0, p, t, s] = first
                    matrix[1, p, t, s] = second
            return carry

        lax.fori_loop(0, states, pack, 0)

    def inner_terms(colour, section):
        other = 1 - colour
        upward = parity == 1 - colour
        for p in range(pairs):
            values = [held[other, p, k] for k in range(states)]
            lower = [pltpu.roll(value, 1, 1) for value in values]
            upper = [pltpu.roll(value, cells_z - 1, 1) for value in values]
            for k in range(states):
                if section == 0:
                    before = lower[k - 1] if k > 0 else 0.0
                    after = upper[k + 1] if k < states - 1 else 0.0
                else:
                    before = held[colour, p, k, :, 0:1] if k > 0 else 0.0
                    after = 0.0
                total = values[k]
                total += jnp.where(wide == 0, before, lower[k])
                total += jnp.where(wide == cells_z - 1, after, upper[k])
                total += jnp.where(tall == 0, 0.0, pltpu.roll(values[k], 1, 0))
                total += jnp.where(tall == cells_y - 1, 0.0, pltpu.roll(values[k], cells_y - 1, 0))
                next_pair = held[other, p + 1, k] if p < pairs - 1 else 0.0
                past_pair = held[other, p - 1, k] if p > 0 else 0.0
                total += jnp.where(upward, next_pair, past_pair)
                if section == 0:
                    total += source[colour, p, k]
                part[p, k] = total

    def halo_terms(colour, half, p, tile):
        lanes = pl.ds(tile * LANES, LANES)
        total = part[p, :, :, lanes]
        upward = jnp.logical_not(even_lanes) if colour == 0 else even_lanes
        if p == 0:
            total += jnp.where(upward, 0.0, halo_x[0, half * has[0], :, :, lanes])
        if p == pairs - 1:
            total += jnp.where(upward, halo_x[1, half * has[1], :, :, lanes], 0.0)
        total += jnp.where(sub == 0, halo_y[0, half * has[2], p, :, :, lanes], 0.0)
        total += jnp.where(sub == cells_y - 1, halo_y[1, half * has[3], p, :, :, lanes], 0.0)
        return total

    def half_sweep(colour, half, section):
        other = 1 - colour
        inner_terms(colour, section)
        wait_received(other, half)
        if colour == 0 and section == 0:
            @pl.when((half == 0) & at_exit)
            def _():
                pltpu.make_async_copy(table, table, interface_sem.at[0]).wait()

                def lay(k, carry):
                    ids = wanted[k]
                    plane = jnp.zeros((cells_y, cells_z), jnp.float32)
                    for g in range(slots):
                        row = jnp.concatenate([table[g]] * (cells_z // LANES), axis=1)
                        plane = jnp.where(ids == float(g), row, plane)
                    halo_x[1, 0, k] = plane
                    return carry

                lax.fori_loop(0, states, lay, 0)

        if colour == 0 and section == 1:
            @pl.when(half == 0)
            def _():
                pltpu.make_async_copy(arrived, arrived, interface_sem.at[1]).wait()
                row = arrived[0]
                for j in range(1, n_gy):
                    row = row + arrived[j]
                columns = [
                    jnp.sum(
                        jnp.where(lane % BLK == x * cells_y + sub, row, 0.0), axis=1, keepdims=True
                    )
                    for x in range(cells_x)
                ]
                for p in range(pairs):
                    for c in range(2):
                        cell = jnp.where(sub % 2 == c, columns[2 * p], columns[2 * p + 1])
                        inflow[c, p] = jnp.where(lane == 0, cell, 0.0)

        for p in range(pairs):
            for tile in range(cells_z // LANES):
                lanes = pl.ds(tile * LANES, LANES)
                total = halo_terms(colour, half, p, tile)
                if section == 0:
                    held[colour, p, :, :, lanes] = total * scale[colour, p, :, :, lanes]
                    continue
                result = None
                for t in range(states):
                    summed = total[t]
                    if t == 0 and tile == 0:
                        summed = summed + inflow[colour, p]
                    driving = source[colour, p, t, :, lanes] + coupling[t] * summed
                    term = matrix[colour, p, t, :, :, lanes] * driving
                    result = term if result is None else result + term
                held[colour, p, :, :, lanes] = result
            if p == 0:
                pl.when(half < halves - 1)(lambda: send((0,), colour, half + 1))

        @pl.when(half < halves - 1)
        def _():
            send((1,), colour, half + 1)
            stage_y(colour)
            send((2, 3), colour, half + 1)

        wait_sent(other, half)

    for section in range(2):
        @pl.when(sa == section)
        def _():
            def sweep(index, carry):
                half_sweep(0, 2 * index, section)
                half_sweep(1, 2 * index + 1, section)
                return carry

            lax.fori_loop(0, SWEEPS, sweep, 0)

    for k in range(states):
        for p in range(pairs):
            first, second = split(held[0, p, k], held[1, p, k])
            out[0, k, 2 * p] = first
            out[0, k, 2 * p + 1] = second

    @pl.when(turbine)
    def _():
        for j in range(n_gy):
            inlet_copy(j).wait_send()

    @pl.when(at_exit)
    def _():
        for g in range(slots):
            row_copy(g).wait_send()


def shards(n_gx, n_gy, fields, sources, diagonal, block_inverse, coupling, donors, returns):
    _, states, cells_x, cells_y, cells_z = fields.shape
    pairs = cells_x // 2
    slots = donors.shape[0]
    assert cells_x % 2 == 0 and cells_y % 2 == 0 and cells_x * cells_y == BLK
    assert cells_y * cells_z == LANES * BLK and slots == n_gx * n_gy
    f32 = jnp.float32
    block = (states, cells_x, cells_y, cells_z)
    halves = 2 * SWEEPS
    anywhere = pl.BlockSpec(memory_space=pl.ANY)
    vmem = pl.BlockSpec(memory_space=pltpu.VMEM)
    smem = pl.BlockSpec(memory_space=pltpu.SMEM)
    by_colour = (2, pairs, states, cells_y, cells_z)
    return pl.pallas_call(
        functools.partial(kernel, n_gx, n_gy, block),
        out_shape=jax.ShapeDtypeStruct(fields.shape, f32),
        in_specs=[anywhere, anywhere, anywhere, anywhere, smem, smem, vmem],
        out_specs=vmem,
        scratch_shapes=[
            pltpu.VMEM(block, f32),
            pltpu.VMEM(block, f32),
            pltpu.VMEM(block, f32),
            pltpu.VMEM((states,) + block, f32),
            pltpu.VMEM(by_colour, f32),
            pltpu.VMEM(by_colour, f32),
            pltpu.VMEM(by_colour, f32),
            pltpu.VMEM((2, pairs, states, states, cells_y, cells_z), f32),
            pltpu.VMEM(by_colour[1:], f32),
            pltpu.VMEM((2, halves, states, cells_y, cells_z), f32),
            pltpu.VMEM((2, halves, pairs, states, 1, cells_z), f32),
            pltpu.VMEM((2, 2, pairs, states, 1, cells_z), f32),
            pltpu.VMEM((2, pairs, cells_y, LANES), f32),
            pltpu.VMEM((states, cells_y, cells_z), f32),
            pltpu.VMEM((slots, 1, LANES), f32),
            pltpu.VMEM((slots, 1, LANES), f32),
            pltpu.VMEM((1, 1, LANES), f32),
            pltpu.VMEM((n_gy, 1, LANES), f32),
            pltpu.SemaphoreType.DMA((4,)),
            pltpu.SemaphoreType.DMA((4, halves)),
            pltpu.SemaphoreType.DMA((4, halves)),
            pltpu.SemaphoreType.DMA((slots,)),
            pltpu.SemaphoreType.DMA((2,)),
        ],
        compiler_params=pltpu.CompilerParams(
            collective_id=0, has_side_effects=True, vmem_limit_bytes=32 * 1024 * 1024
        ),
    )(fields, sources, diagonal, block_inverse, coupling, donors, returns)


def solution(mesh):
    return jax.shard_map(
        functools.partial(shards, mesh.shape["gx"], mesh.shape["gy"]),
        mesh=mesh,
        in_specs=(
            P("sa", None, "gx", "gy", None),
            P("sa", None, "gx", "gy", None),
            P(None, "gx", "gy", None),
            P(None, None, "gx", "gy", None),
            P(),
            P(),
            P("gy", None),
        ),
        out_specs=P("sa", None, "gx", "gy", None),
        check_vma=False,
    )
```

time: 310 us -> 43.5 us (0.14)
  the two profiles are of different devices: /device:TPU:6 before, /device:TPU:3 now
where the time goes in v1:
time: 43.5 us; the launch traced here: 43.2 us
  Pallas kernels  35.3 us (81%)
  local copies, waits for them, and re-layouts  7.83 us (18%)
    pallas_call x1, Pallas kernels, shards(): pl.pallas_call(functools.partial(kernel, n_gx, n_gy, block), out_shape=ja...  35.3 us
    unnamed x14, local copies, waits for them, and re-layouts  7.83 us

profile of v1, /device:TPU:3, one launch (start us, length us, event | category | flops | bytes accessed | tf_op | source)
XLA Modules:
  0.0 43.2 jit_solution(11464110819099021183)
XLA Ops:
  0.0 0.8 %copy.8.donors = s32[16,3]{1,0:T(8,128)S(1)} copy(s32[16,3]{0,1:T(4,128)} %param.12) | data formatting | bytes 384 | tf_op args[5]
  0.8 0.0 copy-start
  0.8 1.9 %copy-done = f32[7,7,4,8,512]{4,3,2,1,0:T(8,128)S(1)} copy-done((f32[7,7,4,8,512]{4,3,2,1,0:T(8,128)S(1)}, f32[7,7,4,8,512]{4,3,2,1,0:T(8,128)}, u32[]{:S(2)}) %copy-start) | copy-done | bytes 3211288
  2.7 0.0 copy-start.1
  2.7 1.0 %copy-done.1 = f32[1,7,4,8,512]{4,3,2,1,0:T(8,128)S(1)} copy-done((f32[1,7,4,8,512]{4,3,2,1,0:T(8,128)S(1)}, f32[1,7,4,8,512]{4,3,2,1,0:T(8,128)}, u32[]{:S(2)}) %copy-start.1) | copy-done | bytes 458776
  3.7 0.0 copy-start.2
  3.7 1.0 %copy-done.2 = f32[1,7,4,8,512]{4,3,2,1,0:T(8,128)S(1)} copy-done((f32[1,7,4,8,512]{4,3,2,1,0:T(8,128)S(1)}, f32[1,7,4,8,512]{4,3,2,1,0:T(8,128)}, u32[]{:S(2)}) %copy-start.2) | copy-done | bytes 458776
  4.7 0.0 copy-start.3
  4.7 1.0 %copy-done.3 = f32[7,4,8,512]{3,2,1,0:T(8,128)S(1)} copy-done((f32[7,4,8,512]{3,2,1,0:T(8,128)S(1)}, f32[7,4,8,512]{3,2,1,0:T(8,128)}, u32[]{:S(2)}) %copy-start.3) | copy-done | bytes 458776
  5.7 0.0 copy-start.4
  5.7 0.7 %copy-done.4 = s32[1,896]{1,0:T(1,128)S(1)} copy-done((s32[1,896]{1,0:T(1,128)S(1)}, s32[1,896]{1,0:T(1,128)}, u32[]{:S(2)}) %copy-start.4) | copy-done | bytes 3608
  6.4 0.0 copy-start.5
  6.4 0.7 %copy-done.5 = f32[7]{0:T(128)S(1)} copy-done((f32[7]{0:T(128)S(1)}, f32[7]{0:T(128)}, u32[]{:S(2)}) %copy-start.5) | copy-done | bytes 52
  7.1 35.3 %shard_map.73 = f32[1,7,4,8,512]{4,3,2,1,0:T(8,128)S(1)} custom-call(f32[1,7,4,8,512]{4,3,2,1,0:T(8,128)S(1)} %copy-done.1, f32[1,7,4,8,512]{4,3,2,1,0:T(8,128)S(1)} %copy-done.2, f32[7,4,8,512]{3,2,1,0:T(8,128)S(1)} %copy-done.3, f32[7,7,4,8,512]{4,3,2,1,0:T(8,128)S(1)} %copy-done, f32[7]{0:T(128)S(1)} %copy-done.5, s32[16,3]{1,0:T(8,128)S(1)} %copy.8.donors, ...), custom_call_target="tpu_custom_call" | custom-call | tf_op jit(solution)/shard_map/pallas_call | solution.py:373
  42.4 0.8 %copy.10 = f32[1,7,4,8,512]{4,3,2,1,0:T(8,128)} copy(f32[1,7,4,8,512]{4,3,2,1,0:T(8,128)S(1)} %shard_map.73) | data formatting | bytes 917504
Async XLA Ops:
  0.8 1.9 %copy-start = (f32[7,7,4,8,512]{4,3,2,1,0:T(8,128)S(1)}, f32[7,7,4,8,512]{4,3,2,1,0:T(8,128)}, u32[]{:S(2)}) copy-start(f32[7,7,4,8,512]{4,3,2,1,0:T(8,128)} %inverse.1) | copy-start | bytes 9633796
  2.7 1.0 %copy-start.1 = (f32[1,7,4,8,512]{4,3,2,1,0:T(8,128)S(1)}, f32[1,7,4,8,512]{4,3,2,1,0:T(8,128)}, u32[]{:S(2)}) copy-start(f32[1,7,4,8,512]{4,3,2,1,0:T(8,128)} %fields.1) | copy-start | bytes 1376260
  3.7 1.0 %copy-start.2 = (f32[1,7,4,8,512]{4,3,2,1,0:T(8,128)S(1)}, f32[1,7,4,8,512]{4,3,2,1,0:T(8,128)}, u32[]{:S(2)}) copy-start(f32[1,7,4,8,512]{4,3,2,1,0:T(8,128)} %sources.1) | copy-start | bytes 1376260
  4.7 1.0 %copy-start.3 = (f32[7,4,8,512]{3,2,1,0:T(8,128)S(1)}, f32[7,4,8,512]{3,2,1,0:T(8,128)}, u32[]{:S(2)}) copy-start(f32[7,4,8,512]{3,2,1,0:T(8,128)} %diagonal.1) | copy-start | bytes 1376260
  5.7 0.7 %copy-start.4 = (s32[1,896]{1,0:T(1,128)S(1)}, s32[1,896]{1,0:T(1,128)}, u32[]{:S(2)}) copy-start(s32[1,896]{1,0:T(1,128)} %returns.1) | copy-start | bytes 10756
  6.4 0.7 %copy-start.5 = (f32[7]{0:T(128)S(1)}, f32[7]{0:T(128)}, u32[]{:S(2)}) copy-start(f32[7]{0:T(128)} %coupling.1) | copy-start | bytes 88

commit v2 on v1

--- a/solution.py
+++ b/solution.py
@@ -11,13 +11,15 @@
 BLK = 32
 LANES = 128
 MESH = pl.DeviceIdType.MESH
+CHUNKS = 2
 
 
 def kernel(
     n_gx, n_gy, sizes,
     fields, sources, diagonal, inverse, coupling, donors, returns, out,
-    raw, raw_source, raw_diagonal, raw_inverse, held, source, scale, matrix, part,
-    halo_x, halo_y, edge_y, inflow, wanted, table, rows, inlet, arrived,
+    raw, raw_source, raw_diagonal, raw_inverse, weights, list_of, returned,
+    held, source, scale, matrix, part,
+    halo_x, halo_y, edge_x, edge_y, inflow, wanted, table, rows, inlet, arrived,
     local_sem, send_sem, recv_sem, slot_sem, interface_sem,
 ):
     states, cells_x, cells_y, cells_z = sizes
@@ -25,6 +27,9 @@
     halves = 2 * SWEEPS
     slots = n_gx * n_gy
     per_row = cells_z // BLK
+    packs = (states + 1) // 2
+    tiles = cells_z // LANES
+    chunk_tiles = tiles // CHUNKS
     gx, gy, sa = lax.axis_index("gx"), lax.axis_index("gy"), lax.axis_index("sa")
     own = gx * n_gy + gy
     has = (
@@ -42,8 +47,14 @@
     load_source = pltpu.make_async_copy(sources.at[0], raw_source, local_sem.at[1])
     load_diagonal = pltpu.make_async_copy(diagonal, raw_diagonal, local_sem.at[2])
     load_inverse = pltpu.make_async_copy(inverse, raw_inverse, local_sem.at[3])
+    load_lists = pltpu.make_async_copy(donors, list_of, local_sem.at[4])
+    load_returns = pltpu.make_async_copy(returns, returned, local_sem.at[5])
+    load_weights = pltpu.make_async_copy(coupling, weights, local_sem.at[6])
     load_fields.start()
+    pl.when(at_exit)(load_lists.start)
+    pl.when(at_exit)(load_returns.start)
     load_source.start()
+    pl.when(turbine)(load_weights.start)
     pl.when(combustor)(load_diagonal.start)
     pl.when(turbine)(load_inverse.start)
 
@@ -76,39 +87,49 @@
     def split(even_plane, odd_plane):
         return (jnp.where(even, even_plane, odd_plane), jnp.where(even, odd_plane, even_plane))
 
-    def stage_y(colour):
-        for p in range(pairs):
-            for k in range(states):
-                edge_y[0, colour, p, k] = held[colour, p, k, 0:1, :]
-                edge_y[1, colour, p, k] = held[colour, p, k, cells_y - 1 : cells_y, :]
-
-    def halo_copy(way, colour, half):
-        if way == 0:
-            ends = (held.at[colour, 0], halo_x.at[1, half])
-        elif way == 1:
-            ends = (held.at[colour, pairs - 1], halo_x.at[0, half])
-        else:
-            ends = (edge_y.at[way - 2, colour], halo_y.at[3 - way, half])
+    def pack_x(values, chosen):
+        moved = [pltpu.roll(values[k], 1, 0) for k in range(packs, states)]
+        moved += [values[k] for k in range(states - packs, packs)]
+        return [jnp.where(chosen, values[k], moved[k]) for k in range(packs)]
+
+    def stage(colour, p, tile, values):
+        at = (tile // chunk_tiles, tile % chunk_tiles)
+        faces = [(0, even_lanes == (colour == 0))] if p == 0 else []
+        faces += [(1, even_lanes == (colour == 1))] if p == pairs - 1 else []
+        for way, chosen in faces:
+            for k, packed in enumerate(pack_x(values, chosen)):
+                edge_x[way, colour, at[0], at[1], k] = packed
+        for k in range(states):
+            edge_y[0, colour, at[0], at[1], p, k] = values[k][0:1]
+            edge_y[1, colour, at[0], at[1], p, k] = values[k][cells_y - 1 : cells_y]
+
+    def halo_copy(way, colour, half, chunk):
+        edges, halos = (edge_x, halo_x) if way < 2 else (edge_y, halo_y)
         return pltpu.make_async_remote_copy(
-            src_ref=ends[0],
-            dst_ref=ends[1],
-            send_sem=send_sem.at[way, half],
-            recv_sem=recv_sem.at[way, half],
+            src_ref=edges.at[way % 2, colour, chunk],
+            dst_ref=halos.at[1 - way % 2, half, chunk],
+            send_sem=send_sem.at[way, half, chunk],
+            recv_sem=recv_sem.at[way, half, chunk],
             device_id=peers[way],
             device_id_type=MESH,
         )
 
-    def send(ways, colour, half):
-        for way in ways:
-            pl.when(has[way] == 1)(lambda way=way: halo_copy(way, colour, half).start())
+    def send(colour, half, chunk):
+        for way in range(4):
+            pl.when(has[way] == 1)(lambda way=way: halo_copy(way, colour, half, chunk).start())
 
     def wait_sent(colour, half):
         for way in range(4):
-            pl.when(has[way] == 1)(lambda way=way: halo_copy(way, colour, half).wait_send())
-
-    def wait_received(colour, half):
+            @pl.when(has[way] == 1)
+            def _():
+                for chunk in range(CHUNKS):
+                    halo_copy(way, colour, half, chunk).wait_send()
+
+    def wait_received(colour, half, chunk):
         for way in range(4):
-            pl.when(has[way] == 1)(lambda way=way: halo_copy(way ^ 1, colour, half).wait_recv())
+            pl.when(has[way] == 1)(
+                lambda way=way: halo_copy(way ^ 1, colour, half, chunk).wait_recv()
+            )
 
     def inlet_copy(j):
         return pltpu.make_async_remote_copy(
@@ -132,22 +153,25 @@
 
     @pl.when(has[0] == 0)
     def _():
-        halo_x[0, 0] = jnp.zeros((states, cells_y, cells_z), jnp.float32)
+        halo_x[0, 0:2] = jnp.zeros((2,) + halo_x.shape[2:], jnp.float32)
 
     @pl.when((has[1] == 0) & turbine)
     def _():
-        halo_x[1, 0] = jnp.zeros((states, cells_y, cells_z), jnp.float32)
+        halo_x[1, 0:2] = jnp.zeros((2,) + halo_x.shape[2:], jnp.float32)
 
     for side in range(2):
         @pl.when(has[2 + side] == 0)
         def _():
-            halo_y[side, 0] = jnp.zeros((pairs, states, 1, cells_z), jnp.float32)
+            halo_y[side, 0:2] = jnp.zeros((2,) + halo_y.shape[2:], jnp.float32)
 
     load_fields.wait()
     for k in range(states):
         for p in range(pairs):
             held[0, p, k], held[1, p, k] = split(raw[k, 2 * p], raw[k, 2 * p + 1])
-    stage_y(1)
+    for tile in range(tiles):
+        lanes = pl.ds(tile * LANES, LANES)
+        for p in range(pairs):
+            stage(1, p, tile, [held[1, p, k, :, lanes] for k in range(states)])
 
     @pl.when(turbine)
     def _():
@@ -158,18 +182,19 @@
 
     @pl.when(at_exit)
     def _():
+        load_lists.wait()
         slot_row = lax.broadcasted_iota(jnp.int32, (slots, LANES), 0)
         in_state = tall * per_row + wide // BLK
 
         def take(e, total):
-            block = jnp.where(donors[e, 0] == gy, donors[e, 1], -1)
+            block = jnp.where(list_of[0, e] == gy, list_of[1, e], -1)
             found = jnp.zeros((cells_y, cells_z), jnp.float32)
             for k in range(states):
                 here = in_state == block - k * (cells_y * per_row)
                 found = jnp.where(here, raw[k, cells_x - 1], found)
             row = jnp.sum(found, axis=0, keepdims=True)
             row = sum(row[:, i * LANES : (i + 1) * LANES] for i in range(cells_z // LANES))
-            return jnp.where(slot_row == donors[e, 2], row, total)
+            return jnp.where(slot_row == list_of[2, e], row, total)
 
         total = lax.fori_loop(0, slots, take, jnp.zeros((slots, LANES), jnp.float32))
         for g in range(slots):
@@ -177,7 +202,8 @@
 
     met = has[0] + has[1] + has[2] + has[3] + sa * n_gy + (1 - sa) * (1 - has[1]) * slots
     pl.semaphore_wait(barrier, met)
-    send(range(4), 1, 0)
+    for chunk in range(CHUNKS):
+        send(1, 0, chunk)
 
     @pl.when(turbine)
     def _():
@@ -192,8 +218,9 @@
         spread_from = lax.broadcasted_iota(jnp.int32, (LANES, cells_z), 0) % per_row
         spread_to = lax.broadcasted_iota(jnp.int32, (LANES, cells_z), 1) // BLK
         spread = jnp.where(spread_from == spread_to, 1.0, 0.0)
+        load_returns.wait()
         for k in range(states):
-            ids = returns[0:1, k * LANES : (k + 1) * LANES].astype(jnp.float32)
+            ids = returned[0:1, k * LANES : (k + 1) * LANES].astype(jnp.float32)
             ids = jnp.where(lane // per_row == sub, ids, 0.0)
             wanted[k] = jnp.dot(
                 ids, spread, precision=lax.Precision.HIGHEST, preferred_element_type=jnp.float32
@@ -215,6 +242,7 @@
 
     @pl.when(turbine)
     def _():
+        load_weights.wait()
         load_inverse.wait()
 
         def pack(s, carry):
@@ -255,20 +283,28 @@
 
     def halo_terms(colour, half, p, tile):
         lanes = pl.ds(tile * LANES, LANES)
-        total = part[p, :, :, lanes]
-        upward = jnp.logical_not(even_lanes) if colour == 0 else even_lanes
-        if p == 0:
-            total += jnp.where(upward, 0.0, halo_x[0, half * has[0], :, :, lanes])
-        if p == pairs - 1:
-            total += jnp.where(upward, halo_x[1, half * has[1], :, :, lanes], 0.0)
-        total += jnp.where(sub == 0, halo_y[0, half * has[2], p, :, :, lanes], 0.0)
-        total += jnp.where(sub == cells_y - 1, halo_y[1, half * has[3], p, :, :, lanes], 0.0)
-        return total
+        at = (tile // chunk_tiles, tile % chunk_tiles)
+        totals = [part[p, k, :, lanes] for k in range(states)]
+        upward = even_lanes == (colour == 1)
+        slot = [half * there + colour * (1 - there) for there in has]
+        for side in ([0] if p == 0 else []) + ([1] if p == pairs - 1 else []):
+            for k in range(packs):
+                packed = halo_x[side, slot[side], at[0], at[1], k]
+                chosen = upward if side == 1 else jnp.logical_not(upward)
+                totals[k] += jnp.where(chosen, packed, 0.0)
+                if k + packs < states:
+                    back = pltpu.roll(packed, cells_y - 1, 0)
+                    totals[k + packs] += jnp.where(chosen, back, 0.0)
+        for k in range(states):
+            below = halo_y[0, slot[2], at[0], at[1], p, k]
+            above = halo_y[1, slot[3], at[0], at[1], p, k]
+            totals[k] += jnp.where(sub == 0, below, jnp.where(sub == cells_y - 1, above, 0.0))
+        return totals
 
     def half_sweep(colour, half, section):
         other = 1 - colour
         inner_terms(colour, section)
-        wait_received(other, half)
+        wait_received(other, half, 0)
         if colour == 0 and section == 0:
             @pl.when((half == 0) & at_exit)
             def _():
@@ -280,10 +316,16 @@
                     for g in range(slots):
                         row = jnp.concatenate([table[g]] * (cells_z // LANES), axis=1)
                         plane = jnp.where(ids == float(g), row, plane)
-                    halo_x[1, 0, k] = plane
+                    wanted[k] = plane
                     return carry
 
                 lax.fori_loop(0, states, lay, 0)
+                for tile in range(tiles):
+                    lanes = pl.ds(tile * LANES, LANES)
+                    planes = [wanted[k, :, lanes] for k in range(states)]
+                    for c in range(2):
+                        for k, packed in enumerate(pack_x(planes, even_lanes == (c == 1))):
+                            halo_x[1, c, tile // chunk_tiles, tile % chunk_tiles, k] = packed
 
         if colour == 0 and section == 1:
             @pl.when(half == 0)
@@ -303,30 +345,28 @@
                         cell = jnp.where(sub % 2 == c, columns[2 * p], columns[2 * p + 1])
                         inflow[c, p] = jnp.where(lane == 0, cell, 0.0)
 
-        for p in range(pairs):
-            for tile in range(cells_z // LANES):
+        for chunk in range(CHUNKS):
+            if chunk > 0:
+                wait_received(other, half, chunk)
+            for tile in range(chunk * chunk_tiles, (chunk + 1) * chunk_tiles):
                 lanes = pl.ds(tile * LANES, LANES)
-                total = halo_terms(colour, half, p, tile)
-                if section == 0:
-                    held[colour, p, :, :, lanes] = total * scale[colour, p, :, :, lanes]
-                    continue
-                result = None
-                for t in range(states):
-                    summed = total[t]
-                    if t == 0 and tile == 0:
-                        summed = summed + inflow[colour, p]
-                    driving = source[colour, p, t, :, lanes] + coupling[t] * summed
-                    term = matrix[colour, p, t, :, :, lanes] * driving
-                    result = term if result is None else result + term
-                held[colour, p, :, :, lanes] = result
-            if p == 0:
-                pl.when(half < halves - 1)(lambda: send((0,), colour, half + 1))
-
-        @pl.when(half < halves - 1)
-        def _():
-            send((1,), colour, half + 1)
-            stage_y(colour)
-            send((2, 3), colour, half + 1)
+                for p in range(pairs):
+                    totals = halo_terms(colour, half, p, tile)
+                    if section == 0:
+                        results = [totals[k] * scale[colour, p, k, :, lanes] for k in range(states)]
+                    else:
+                        if tile == 0:
+                            totals[0] += inflow[colour, p]
+                        result = None
+                        for t in range(states):
+                            driving = source[colour, p, t, :, lanes] + weights[t] * totals[t]
+                            term = matrix[colour, p, t, :, :, lanes] * driving
+                            result = term if result is None else result + term
+                        results = [result[k] for k in range(states)]
+                    for k in range(states):
+                        held[colour, p, k, :, lanes] = results[k]
+                    stage(colour, p, tile, results)
+            pl.when(half < halves - 1)(functools.partial(send, colour, half + 1, chunk))
 
         wait_sent(other, half)
 
@@ -366,44 +406,50 @@
     f32 = jnp.float32
     block = (states, cells_x, cells_y, cells_z)
     halves = 2 * SWEEPS
-    anywhere = pl.BlockSpec(memory_space=pl.ANY)
+    tiles = cells_z // LANES
+    packs = (states + 1) // 2
+    chunk = (CHUNKS, tiles // CHUNKS)
+    hbm = pl.BlockSpec(memory_space=pltpu.HBM)
     vmem = pl.BlockSpec(memory_space=pltpu.VMEM)
-    smem = pl.BlockSpec(memory_space=pltpu.SMEM)
     by_colour = (2, pairs, states, cells_y, cells_z)
     return pl.pallas_call(
         functools.partial(kernel, n_gx, n_gy, block),
         out_shape=jax.ShapeDtypeStruct(fields.shape, f32),
-        in_specs=[anywhere, anywhere, anywhere, anywhere, smem, smem, vmem],
+        in_specs=[hbm] * 7,
         out_specs=vmem,
         scratch_shapes=[
             pltpu.VMEM(block, f32),
             pltpu.VMEM(block, f32),
             pltpu.VMEM(block, f32),
             pltpu.VMEM((states,) + block, f32),
+            pltpu.SMEM(coupling.shape, f32),
+            pltpu.SMEM(donors.shape[::-1], jnp.int32),
+            pltpu.VMEM(returns.shape, jnp.int32),
             pltpu.VMEM(by_colour, f32),
             pltpu.VMEM(by_colour, f32),
             pltpu.VMEM(by_colour, f32),
             pltpu.VMEM((2, pairs, states, states, cells_y, cells_z), f32),
             pltpu.VMEM(by_colour[1:], f32),
-            pltpu.VMEM((2, halves, states, cells_y, cells_z), f32),
-            pltpu.VMEM((2, halves, pairs, states, 1, cells_z), f32),
-            pltpu.VMEM((2, 2, pairs, states, 1, cells_z), f32),
+            pltpu.VMEM((2, halves) + chunk + (packs, cells_y, LANES), f32),
+            pltpu.VMEM((2, halves) + chunk + (pairs, states, 1, LANES), f32),
+            pltpu.VMEM((2, 2) + chunk + (packs, cells_y, LANES), f32),
+            pltpu.VMEM((2, 2) + chunk + (pairs, states, 1, LANES), f32),
             pltpu.VMEM((2, pairs, cells_y, LANES), f32),
             pltpu.VMEM((states, cells_y, cells_z), f32),
             pltpu.VMEM((slots, 1, LANES), f32),
             pltpu.VMEM((slots, 1, LANES), f32),
             pltpu.VMEM((1, 1, LANES), f32),
             pltpu.VMEM((n_gy, 1, LANES), f32),
-            pltpu.SemaphoreType.DMA((4,)),
-            pltpu.SemaphoreType.DMA((4, halves)),
-            pltpu.SemaphoreType.DMA((4, halves)),
+            pltpu.SemaphoreType.DMA((7,)),
+            pltpu.SemaphoreType.DMA((4, halves, CHUNKS)),
+            pltpu.SemaphoreType.DMA((4, halves, CHUNKS)),
             pltpu.SemaphoreType.DMA((slots,)),
             pltpu.SemaphoreType.DMA((2,)),
         ],
         compiler_params=pltpu.CompilerParams(
-            collective_id=0, has_side_effects=True, vmem_limit_bytes=32 * 1024 * 1024
+            collective_id=0, has_side_effects=True, vmem_limit_bytes=60 * 1024 * 1024
         ),
-    )(fields, sources, diagonal, block_inverse, coupling, donors, returns)
+    )(fields, sources, diagonal, block_inverse, coupling, donors.T, returns)
 
 
 def solution(mesh):

time: 43.5 us -> 33.3 us (0.77)
  local copies, waits for them, and re-layouts: 7.83 us -> 1.83 us
  Pallas kernels: 35.3 us -> 31.3 us
    unnamed x14 -> x1, local copies, waits for them, and re-layouts: 7.83 us -> 1.83 us
    pallas_call x1, Pallas kernels: 35.3 us -> 31.3 us  [shards(): pl.pallas_call(functools.partial(kernel, n_gx, n_gy, block), out_shape=ja...]
where the time goes in v2:
time: 33.3 us; the launch traced here: 33.1 us
  Pallas kernels  31.3 us (94%)
  local copies, waits for them, and re-layouts  1.83 us (5%)
    pallas_call x1, Pallas kernels, shards(): pl.pallas_call(functools.partial(kernel, n_gx, n_gy, block), out_shape=ja...  31.3 us
    unnamed x1, local copies, waits for them, and re-layouts  1.83 us

profile of v2, /device:TPU:3, one launch (start us, length us, event | category | flops | bytes accessed | tf_op | source)
XLA Modules:
  0.0 33.1 jit_solution(11697178615089493949)
XLA Ops:
  0.0 31.3 %shard_map.73 = f32[1,7,4,8,512]{4,3,2,1,0:T(8,128)} custom-call(f32[1,7,4,8,512]{4,3,2,1,0:T(8,128)} %fields.1, f32[1,7,4,8,512]{4,3,2,1,0:T(8,128)} %sources.1, f32[7,4,8,512]{3,2,1,0:T(8,128)} %diagonal.1, f32[7,7,4,8,512]{4,3,2,1,0:T(8,128)} %inverse.1, f32[7]{0:T(128)} %coupling.1, s32[3,16]{1,0:T(4,128)} %bitcast.1, s32[1,896]{1,0:T(1,128)} %returns.1), custom_call_target="tpu_custom_call" | custom-call | tf_op jit(solution)/shard_map/pallas_call | solution.py:415
  31.3 1.8 %copy.9 = f32[1,7,4,8,512]{4,3,2,1,0:T(8,128)} copy(f32[1,7,4,8,512]{4,3,2,1,0:T(8,128)} %shard_map.73) | data formatting | bytes 917504

commit v3 on v2

--- a/solution.py
+++ b/solution.py
@@ -12,6 +12,8 @@
 LANES = 128
 MESH = pl.DeviceIdType.MESH
 CHUNKS = 2
+X_WAYS, Y_WAYS = (0, 1), (2, 3)
+PLANES = ((0, 3), (2, 1))
 
 
 def kernel(
@@ -23,7 +25,7 @@
     local_sem, send_sem, recv_sem, slot_sem, interface_sem,
 ):
     states, cells_x, cells_y, cells_z = sizes
-    pairs = cells_x // 2
+    pairs = len(PLANES)
     halves = 2 * SWEEPS
     slots = n_gx * n_gy
     per_row = cells_z // BLK
@@ -87,48 +89,53 @@
     def split(even_plane, odd_plane):
         return (jnp.where(even, even_plane, odd_plane), jnp.where(even, odd_plane, even_plane))
 
-    def pack_x(values, chosen):
+    def split_planes(block, k, p):
+        return split(block[k, PLANES[p][0]], block[k, PLANES[p][1]])
+
+    def pack_x(values, *choices):
         moved = [pltpu.roll(values[k], 1, 0) for k in range(packs, states)]
         moved += [values[k] for k in range(states - packs, packs)]
-        return [jnp.where(chosen, values[k], moved[k]) for k in range(packs)]
+        return [
+            [jnp.where(chosen, values[k], moved[k]) for k in range(packs)] for chosen in choices
+        ]
 
     def stage(colour, p, tile, values):
-        at = (tile // chunk_tiles, tile % chunk_tiles)
-        faces = [(0, even_lanes == (colour == 0))] if p == 0 else []
-        faces += [(1, even_lanes == (colour == 1))] if p == pairs - 1 else []
-        for way, chosen in faces:
-            for k, packed in enumerate(pack_x(values, chosen)):
-                edge_x[way, colour, at[0], at[1], k] = packed
+        if p == 0:
+            faces = pack_x(values, even_lanes == (colour == 0), even_lanes == (colour == 1))
+            for way in range(2):
+                for k in range(packs):
+                    at = (tile // chunk_tiles, tile % chunk_tiles)
+                    edge_x[way, colour, at[0], at[1], k] = faces[way][k]
         for k in range(states):
-            edge_y[0, colour, at[0], at[1], p, k] = values[k][0:1]
-            edge_y[1, colour, at[0], at[1], p, k] = values[k][cells_y - 1 : cells_y]
-
-    def halo_copy(way, colour, half, chunk):
+            edge_y[0, colour, p, tile, k] = values[k][0:1]
+            edge_y[1, colour, p, tile, k] = values[k][cells_y - 1 : cells_y]
+
+    def halo_copy(way, colour, half, piece):
         edges, halos = (edge_x, halo_x) if way < 2 else (edge_y, halo_y)
         return pltpu.make_async_remote_copy(
-            src_ref=edges.at[way % 2, colour, chunk],
-            dst_ref=halos.at[1 - way % 2, half, chunk],
-            send_sem=send_sem.at[way, half, chunk],
-            recv_sem=recv_sem.at[way, half, chunk],
+            src_ref=edges.at[way % 2, colour, piece],
+            dst_ref=halos.at[1 - way % 2, half, piece],
+            send_sem=send_sem.at[way, half, piece],
+            recv_sem=recv_sem.at[way, half, piece],
             device_id=peers[way],
             device_id_type=MESH,
         )
 
-    def send(colour, half, chunk):
-        for way in range(4):
-            pl.when(has[way] == 1)(lambda way=way: halo_copy(way, colour, half, chunk).start())
+    def send(ways, colour, half, piece):
+        for way in ways:
+            pl.when(has[way] == 1)(lambda way=way: halo_copy(way, colour, half, piece).start())
 
     def wait_sent(colour, half):
         for way in range(4):
             @pl.when(has[way] == 1)
             def _():
-                for chunk in range(CHUNKS):
-                    halo_copy(way, colour, half, chunk).wait_send()
-
-    def wait_received(colour, half, chunk):
-        for way in range(4):
+                for piece in range(CHUNKS if way < 2 else pairs):
+                    halo_copy(way, colour, half, piece).wait_send()
+
+    def wait_received(ways, colour, half, piece):
+        for way in ways:
             pl.when(has[way] == 1)(
-                lambda way=way: halo_copy(way ^ 1, colour, half, chunk).wait_recv()
+                lambda way=way: halo_copy(way ^ 1, colour, half, piece).wait_recv()
             )
 
     def inlet_copy(j):
@@ -167,7 +174,7 @@
     load_fields.wait()
     for k in range(states):
         for p in range(pairs):
-            held[0, p, k], held[1, p, k] = split(raw[k, 2 * p], raw[k, 2 * p + 1])
+            held[0, p, k], held[1, p, k] = split_planes(raw, k, p)
     for tile in range(tiles):
         lanes = pl.ds(tile * LANES, LANES)
         for p in range(pairs):
@@ -203,7 +210,9 @@
     met = has[0] + has[1] + has[2] + has[3] + sa * n_gy + (1 - sa) * (1 - has[1]) * slots
     pl.semaphore_wait(barrier, met)
     for chunk in range(CHUNKS):
-        send(1, 0, chunk)
+        send(X_WAYS, 1, 0, chunk)
+    for p in range(pairs):
+        send(Y_WAYS, 1, 0, p)
 
     @pl.when(turbine)
     def _():
@@ -229,14 +238,14 @@
     load_source.wait()
     for k in range(states):
         for p in range(pairs):
-            source[0, p, k], source[1, p, k] = split(raw_source[k, 2 * p], raw_source[k, 2 * p + 1])
+            source[0, p, k], source[1, p, k] = split_planes(raw_source, k, p)
 
     @pl.when(combustor)
     def _():
         load_diagonal.wait()
         for k in range(states):
             for p in range(pairs):
-                first, second = split(raw_diagonal[k, 2 * p], raw_diagonal[k, 2 * p + 1])
+                first, second = split_planes(raw_diagonal, k, p)
                 scale[0, p, k] = 1.0 / (6.0 + first)
                 scale[1, p, k] = 1.0 / (6.0 + second)
 
@@ -248,7 +257,7 @@
         def pack(s, carry):
             for t in range(states):
                 for p in range(pairs):
-                    first, second = split(raw_inverse[s, t, 2 * p], raw_inverse[s, t, 2 * p + 1])
+                    first, second = split_planes(raw_inverse.at[s], t, p)
                     matrix[0, p, t, s] = first
                     matrix[1, p, t, s] = second
             return carry
@@ -257,7 +266,6 @@
 
     def inner_terms(colour, section):
         other = 1 - colour
-        upward = parity == 1 - colour
         for p in range(pairs):
             values = [held[other, p, k] for k in range(states)]
             lower = [pltpu.roll(value, 1, 1) for value in values]
@@ -269,14 +277,13 @@
                 else:
                     before = held[colour, p, k, :, 0:1] if k > 0 else 0.0
                     after = 0.0
-                total = values[k]
+                total = held[other, 1, k]
+                if p == 1:
+                    total += held[other, 0, k]
                 total += jnp.where(wide == 0, before, lower[k])
                 total += jnp.where(wide == cells_z - 1, after, upper[k])
                 total += jnp.where(tall == 0, 0.0, pltpu.roll(values[k], 1, 0))
                 total += jnp.where(tall == cells_y - 1, 0.0, pltpu.roll(values[k], cells_y - 1, 0))
-                next_pair = held[other, p + 1, k] if p < pairs - 1 else 0.0
-                past_pair = held[other, p - 1, k] if p > 0 else 0.0
-                total += jnp.where(upward, next_pair, past_pair)
                 if section == 0:
                     total += source[colour, p, k]
                 part[p, k] = total
@@ -287,24 +294,23 @@
         totals = [part[p, k, :, lanes] for k in range(states)]
         upward = even_lanes == (colour == 1)
         slot = [half * there + colour * (1 - there) for there in has]
-        for side in ([0] if p == 0 else []) + ([1] if p == pairs - 1 else []):
-            for k in range(packs):
-                packed = halo_x[side, slot[side], at[0], at[1], k]
-                chosen = upward if side == 1 else jnp.logical_not(upward)
-                totals[k] += jnp.where(chosen, packed, 0.0)
-                if k + packs < states:
-                    back = pltpu.roll(packed, cells_y - 1, 0)
-                    totals[k + packs] += jnp.where(chosen, back, 0.0)
+        for k in range(packs if p == 0 else 0):
+            below = halo_x[0, slot[0], at[0], at[1], k]
+            above = halo_x[1, slot[1], at[0], at[1], k]
+            totals[k] += jnp.where(upward, above, below)
+            if k + packs < states:
+                totals[k + packs] += pltpu.roll(jnp.where(upward, below, above), cells_y - 1, 0)
         for k in range(states):
-            below = halo_y[0, slot[2], at[0], at[1], p, k]
-            above = halo_y[1, slot[3], at[0], at[1], p, k]
+            below = halo_y[0, slot[2], p, tile, k]
+            above = halo_y[1, slot[3], p, tile, k]
             totals[k] += jnp.where(sub == 0, below, jnp.where(sub == cells_y - 1, above, 0.0))
         return totals
 
     def half_sweep(colour, half, section):
         other = 1 - colour
         inner_terms(colour, section)
-        wait_received(other, half, 0)
+        wait_received(X_WAYS, other, half, 0)
+        wait_received(Y_WAYS, other, half, 0)
         if colour == 0 and section == 0:
             @pl.when((half == 0) & at_exit)
             def _():
@@ -324,7 +330,7 @@
                     lanes = pl.ds(tile * LANES, LANES)
                     planes = [wanted[k, :, lanes] for k in range(states)]
                     for c in range(2):
-                        for k, packed in enumerate(pack_x(planes, even_lanes == (c == 1))):
+                        for k, packed in enumerate(pack_x(planes, even_lanes == (c == 1))[0]):
                             halo_x[1, c, tile // chunk_tiles, tile % chunk_tiles, k] = packed
 
         if colour == 0 and section == 1:
@@ -342,31 +348,39 @@
                 ]
                 for p in range(pairs):
                     for c in range(2):
-                        cell = jnp.where(sub % 2 == c, columns[2 * p], columns[2 * p + 1])
+                        cell = jnp.where(sub % 2 == c, columns[PLANES[p][0]], columns[PLANES[p][1]])
                         inflow[c, p] = jnp.where(lane == 0, cell, 0.0)
 
+        def update(p, tile):
+            lanes = pl.ds(tile * LANES, LANES)
+            totals = halo_terms(colour, half, p, tile)
+            if section == 0:
+                results = [totals[k] * scale[colour, p, k, :, lanes] for k in range(states)]
+            else:
+                if tile == 0:
+                    totals[0] += inflow[colour, p]
+                result = None
+                for t in range(states):
+                    driving = source[colour, p, t, :, lanes] + weights[t] * totals[t]
+                    term = matrix[colour, p, t, :, :, lanes] * driving
+                    result = term if result is None else result + term
+                results = [result[k] for k in range(states)]
+            for k in range(states):
+                held[colour, p, k, :, lanes] = results[k]
+            stage(colour, p, tile, results)
+
+        going_on = pl.when(half < halves - 1)
         for chunk in range(CHUNKS):
             if chunk > 0:
-                wait_received(other, half, chunk)
+                wait_received(X_WAYS, other, half, chunk)
             for tile in range(chunk * chunk_tiles, (chunk + 1) * chunk_tiles):
-                lanes = pl.ds(tile * LANES, LANES)
-                for p in range(pairs):
-                    totals = halo_terms(colour, half, p, tile)
-                    if section == 0:
-                        results = [totals[k] * scale[colour, p, k, :, lanes] for k in range(states)]
-                    else:
-                        if tile == 0:
-                            totals[0] += inflow[colour, p]
-                        result = None
-                        for t in range(states):
-                            driving = source[colour, p, t, :, lanes] + weights[t] * totals[t]
-                            term = matrix[colour, p, t, :, :, lanes] * driving
-                            result = term if result is None else result + term
-                        results = [result[k] for k in range(states)]
-                    for k in range(states):
-                        held[colour, p, k, :, lanes] = results[k]
-                    stage(colour, p, tile, results)
-            pl.when(half < halves - 1)(functools.partial(send, colour, half + 1, chunk))
+                update(0, tile)
+            going_on(functools.partial(send, X_WAYS, colour, half + 1, chunk))
+        going_on(functools.partial(send, Y_WAYS, colour, half + 1, 0))
+        wait_received(Y_WAYS, other, half, 1)
+        for tile in range(tiles):
+            update(1, tile)
+        going_on(functools.partial(send, Y_WAYS, colour, half + 1, 1))
 
         wait_sent(other, half)
 
@@ -383,8 +397,8 @@
     for k in range(states):
         for p in range(pairs):
             first, second = split(held[0, p, k], held[1, p, k])
-            out[0, k, 2 * p] = first
-            out[0, k, 2 * p + 1] = second
+            out[0, k, PLANES[p][0]] = first
+            out[0, k, PLANES[p][1]] = second
 
     @pl.when(turbine)
     def _():
@@ -399,9 +413,9 @@
 
 def shards(n_gx, n_gy, fields, sources, diagonal, block_inverse, coupling, donors, returns):
     _, states, cells_x, cells_y, cells_z = fields.shape
-    pairs = cells_x // 2
+    pairs = len(PLANES)
     slots = donors.shape[0]
-    assert cells_x % 2 == 0 and cells_y % 2 == 0 and cells_x * cells_y == BLK
+    assert cells_x == 4 and cells_y % 2 == 0 and cells_x * cells_y == BLK
     assert cells_y * cells_z == LANES * BLK and slots == n_gx * n_gy
     f32 = jnp.float32
     block = (states, cells_x, cells_y, cells_z)
@@ -431,9 +445,9 @@
             pltpu.VMEM((2, pairs, states, states, cells_y, cells_z), f32),
             pltpu.VMEM(by_colour[1:], f32),
             pltpu.VMEM((2, halves) + chunk + (packs, cells_y, LANES), f32),
-            pltpu.VMEM((2, halves) + chunk + (pairs, states, 1, LANES), f32),
+            pltpu.VMEM((2, halves, pairs, tiles, states, 1, LANES), f32),
             pltpu.VMEM((2, 2) + chunk + (packs, cells_y, LANES), f32),
-            pltpu.VMEM((2, 2) + chunk + (pairs, states, 1, LANES), f32),
+            pltpu.VMEM((2, 2, pairs, tiles, states, 1, LANES), f32),
             pltpu.VMEM((2, pairs, cells_y, LANES), f32),
             pltpu.VMEM((states, cells_y, cells_z), f32),
             pltpu.VMEM((slots, 1, LANES), f32),
@@ -441,8 +455,8 @@
             pltpu.VMEM((1, 1, LANES), f32),
             pltpu.VMEM((n_gy, 1, LANES), f32),
             pltpu.SemaphoreType.DMA((7,)),
-            pltpu.SemaphoreType.DMA((4, halves, CHUNKS)),
-            pltpu.SemaphoreType.DMA((4, halves, CHUNKS)),
+            pltpu.SemaphoreType.DMA((4, halves, max(CHUNKS, pairs))),
+            pltpu.SemaphoreType.DMA((4, halves, max(CHUNKS, pairs))),
             pltpu.SemaphoreType.DMA((slots,)),
             pltpu.SemaphoreType.DMA((2,)),
         ],

time: 33.3 us -> 33.5 us (level)
  no operation moved by 1% of the time
where the time goes in v3:
time: 33.5 us; the launch traced here: 33.3 us
  Pallas kernels  31.5 us (94%)
  local copies, waits for them, and re-layouts  1.83 us (5%)
    pallas_call x1, Pallas kernels, shards(): pl.pallas_call(functools.partial(kernel, n_gx, n_gy, block), out_shape=ja...  31.5 us
    unnamed x1, local copies, waits for them, and re-layouts  1.83 us

profile of v3, /device:TPU:3, one launch (start us, length us, event | category | flops | bytes accessed | tf_op | source)
XLA Modules:
  0.0 33.3 jit_solution(14585901077626834981)
XLA Ops:
  0.0 31.5 %shard_map.73 = f32[1,7,4,8,512]{4,3,2,1,0:T(8,128)} custom-call(f32[1,7,4,8,512]{4,3,2,1,0:T(8,128)} %fields.1, f32[1,7,4,8,512]{4,3,2,1,0:T(8,128)} %sources.1, f32[7,4,8,512]{3,2,1,0:T(8,128)} %diagonal.1, f32[7,7,4,8,512]{4,3,2,1,0:T(8,128)} %inverse.1, f32[7]{0:T(128)} %coupling.1, s32[3,16]{1,0:T(4,128)} %bitcast.1, s32[1,896]{1,0:T(1,128)} %returns.1), custom_call_target="tpu_custom_call" | custom-call | tf_op jit(solution)/shard_map/pallas_call | solution.py:429
  31.5 1.8 %copy.9 = f32[1,7,4,8,512]{4,3,2,1,0:T(8,128)} copy(f32[1,7,4,8,512]{4,3,2,1,0:T(8,128)} %shard_map.73) | data formatting | bytes 917504

commit v4 on v3

--- a/solution.py
+++ b/solution.py
@@ -203,7 +203,7 @@
             row = sum(row[:, i * LANES : (i + 1) * LANES] for i in range(cells_z // LANES))
             return jnp.where(slot_row == list_of[2, e], row, total)
 
-        total = lax.fori_loop(0, slots, take, jnp.zeros((slots, LANES), jnp.float32))
+        total = lax.fori_loop(0, slots, take, jnp.zeros((slots, LANES), jnp.float32), unroll=4)
         for g in range(slots):
             rows[g] = total[g : g + 1]
 
@@ -232,7 +232,7 @@
             ids = returned[0:1, k * LANES : (k + 1) * LANES].astype(jnp.float32)
             ids = jnp.where(lane // per_row == sub, ids, 0.0)
             wanted[k] = jnp.dot(
-                ids, spread, precision=lax.Precision.HIGHEST, preferred_element_type=jnp.float32
+                ids, spread, preferred_element_type=jnp.float32
             )
 
     load_source.wait()
@@ -423,6 +423,10 @@
     tiles = cells_z // LANES
     packs = (states + 1) // 2
     chunk = (CHUNKS, tiles // CHUNKS)
+    operands = [
+        pltpu.with_memory_space_constraint(operand, pltpu.HBM)
+        for operand in (fields, sources, diagonal, block_inverse, coupling, donors.T, returns)
+    ]
     hbm = pl.BlockSpec(memory_space=pltpu.HBM)
     vmem = pl.BlockSpec(memory_space=pltpu.VMEM)
     by_colour = (2, pairs, states, cells_y, cells_z)
@@ -461,9 +465,9 @@
             pltpu.SemaphoreType.DMA((2,)),
         ],
         compiler_params=pltpu.CompilerParams(
-            collective_id=0, has_side_effects=True, vmem_limit_bytes=60 * 1024 * 1024
+            collective_id=0, has_side_effects=True, vmem_limit_bytes=32 * 1024 * 1024
         ),
-    )(fields, sources, diagonal, block_inverse, coupling, donors.T, returns)
+    )(*operands)
 
 
 def solution(mesh):

time: 33.5 us -> 31.7 us (0.946)
  local copies, waits for them, and re-layouts: 1.83 us -> 0.77 us
  Pallas kernels: 31.5 us -> 30.8 us
    unnamed x1, local copies, waits for them, and re-layouts: 1.83 us -> 0.77 us
    pallas_call x1, Pallas kernels: 31.5 us -> 30.8 us  [shards(): pl.pallas_call(functools.partial(kernel, n_gx, n_gy, block), out_shape=ja...]
where the time goes in v4:
time: 31.7 us; the launch traced here: 31.6 us
  Pallas kernels  30.8 us (97%)
  local copies, waits for them, and re-layouts  0.77 us (2%)
    pallas_call x1, Pallas kernels, shards(): pl.pallas_call(functools.partial(kernel, n_gx, n_gy, block), out_shape=ja...  30.8 us
    unnamed x1, local copies, waits for them, and re-layouts  0.77 us

profile of v4, /device:TPU:3, one launch (start us, length us, event | category | flops | bytes accessed | tf_op | source)
XLA Modules:
  0.0 31.6 jit_solution(7322253987651790071)
XLA Ops:
  0.0 30.8 %shard_map.73 = f32[1,7,4,8,512]{4,3,2,1,0:T(8,128)S(1)} custom-call(f32[1,7,4,8,512]{4,3,2,1,0:T(8,128)} %fields.1, f32[1,7,4,8,512]{4,3,2,1,0:T(8,128)} %sources.1, f32[7,4,8,512]{3,2,1,0:T(8,128)} %diagonal.1, f32[7,7,4,8,512]{4,3,2,1,0:T(8,128)} %inverse.1, f32[7]{0:T(128)} %coupling.1, s32[3,16]{1,0:T(4,128)} %bitcast.1, s32[1,896]{1,0:T(1,128)} %returns.1), custom_call_target="tpu_custom_call" | custom-call | tf_op jit(solution)/shard_map/pallas_call | solution.py:433
  30.8 0.8 %copy.9 = f32[1,7,4,8,512]{4,3,2,1,0:T(8,128)} copy(f32[1,7,4,8,512]{4,3,2,1,0:T(8,128)S(1)} %shard_map.73) | data formatting | bytes 917504

commit v5 on v4

--- a/solution.py
+++ b/solution.py
@@ -11,7 +11,7 @@
 BLK = 32
 LANES = 128
 MESH = pl.DeviceIdType.MESH
-CHUNKS = 2
+CHUNKS = 1
 X_WAYS, Y_WAYS = (0, 1), (2, 3)
 PLANES = ((0, 3), (2, 1))
 
@@ -209,10 +209,10 @@
 
     met = has[0] + has[1] + has[2] + has[3] + sa * n_gy + (1 - sa) * (1 - has[1]) * slots
     pl.semaphore_wait(barrier, met)
+    for p in range(pairs):
+        send(Y_WAYS, 1, 0, p)
     for chunk in range(CHUNKS):
         send(X_WAYS, 1, 0, chunk)
-    for p in range(pairs):
-        send(Y_WAYS, 1, 0, p)
 
     @pl.when(turbine)
     def _():
@@ -375,8 +375,9 @@
                 wait_received(X_WAYS, other, half, chunk)
             for tile in range(chunk * chunk_tiles, (chunk + 1) * chunk_tiles):
                 update(0, tile)
+            if chunk == CHUNKS - 1:
+                going_on(functools.partial(send, Y_WAYS, colour, half + 1, 0))
             going_on(functools.partial(send, X_WAYS, colour, half + 1, chunk))
-        going_on(functools.partial(send, Y_WAYS, colour, half + 1, 0))
         wait_received(Y_WAYS, other, half, 1)
         for tile in range(tiles):
             update(1, tile)

time: 31.7 us -> 32 us (level)
    pallas_call x1, Pallas kernels: 30.8 us -> 31.1 us  [shards(): pl.pallas_call(functools.partial(kernel, n_gx, n_gy, block), out_shape=ja...]
where the time goes in v5:
time: 32 us; the launch traced here: 31.9 us
  Pallas kernels  31.1 us (97%)
  local copies, waits for them, and re-layouts  0.77 us (2%)
    pallas_call x1, Pallas kernels, shards(): pl.pallas_call(functools.partial(kernel, n_gx, n_gy, block), out_shape=ja...  31.1 us
    unnamed x1, local copies, waits for them, and re-layouts  0.77 us

profile of v5, /device:TPU:3, one launch (start us, length us, event | category | flops | bytes accessed | tf_op | source)
XLA Modules:
  0.0 31.9 jit_solution(51643481527363837)
XLA Ops:
  0.0 31.1 %shard_map.73 = f32[1,7,4,8,512]{4,3,2,1,0:T(8,128)S(1)} custom-call(f32[1,7,4,8,512]{4,3,2,1,0:T(8,128)} %fields.1, f32[1,7,4,8,512]{4,3,2,1,0:T(8,128)} %sources.1, f32[7,4,8,512]{3,2,1,0:T(8,128)} %diagonal.1, f32[7,7,4,8,512]{4,3,2,1,0:T(8,128)} %inverse.1, f32[7]{0:T(128)} %coupling.1, s32[3,16]{1,0:T(4,128)} %bitcast.1, s32[1,896]{1,0:T(1,128)} %returns.1), custom_call_target="tpu_custom_call" | custom-call | tf_op jit(solution)/shard_map/pallas_call | solution.py:434
  31.1 0.8 %copy.9 = f32[1,7,4,8,512]{4,3,2,1,0:T(8,128)} copy(f32[1,7,4,8,512]{4,3,2,1,0:T(8,128)S(1)} %shard_map.73) | data formatting | bytes 917504

commit v6 on v4

--- a/solution.py
+++ b/solution.py
@@ -209,6 +209,12 @@
 
     met = has[0] + has[1] + has[2] + has[3] + sa * n_gy + (1 - sa) * (1 - has[1]) * slots
     pl.semaphore_wait(barrier, met)
+
+    @pl.when(at_exit)
+    def _():
+        for g in range(slots):
+            row_copy(g).start()
+
     for chunk in range(CHUNKS):
         send(X_WAYS, 1, 0, chunk)
     for p in range(pairs):
@@ -221,9 +227,6 @@
 
     @pl.when(at_exit)
     def _():
-        for g in range(slots):
-            row_copy(g).start()
-
         spread_from = lax.broadcasted_iota(jnp.int32, (LANES, cells_z), 0) % per_row
         spread_to = lax.broadcasted_iota(jnp.int32, (LANES, cells_z), 1) // BLK
         spread = jnp.where(spread_from == spread_to, 1.0, 0.0)
@@ -284,26 +287,25 @@
                 total += jnp.where(wide == cells_z - 1, after, upper[k])
                 total += jnp.where(tall == 0, 0.0, pltpu.roll(values[k], 1, 0))
                 total += jnp.where(tall == cells_y - 1, 0.0, pltpu.roll(values[k], cells_y - 1, 0))
-                if section == 0:
-                    total += source[colour, p, k]
-                part[p, k] = total
+                if section == 1:
+                    total = weights[k] * total
+                part[p, k] = source[colour, p, k] + total
 
     def halo_terms(colour, half, p, tile):
-        lanes = pl.ds(tile * LANES, LANES)
         at = (tile // chunk_tiles, tile % chunk_tiles)
-        totals = [part[p, k, :, lanes] for k in range(states)]
         upward = even_lanes == (colour == 1)
         slot = [half * there + colour * (1 - there) for there in has]
+        totals = []
+        for k in range(states):
+            below = halo_y[0, slot[2], p, tile, k]
+            above = halo_y[1, slot[3], p, tile, k]
+            totals.append(jnp.where(sub == 0, below, jnp.where(sub == cells_y - 1, above, 0.0)))
         for k in range(packs if p == 0 else 0):
             below = halo_x[0, slot[0], at[0], at[1], k]
             above = halo_x[1, slot[1], at[0], at[1], k]
             totals[k] += jnp.where(upward, above, below)
             if k + packs < states:
                 totals[k + packs] += pltpu.roll(jnp.where(upward, below, above), cells_y - 1, 0)
-        for k in range(states):
-            below = halo_y[0, slot[2], p, tile, k]
-            above = halo_y[1, slot[3], p, tile, k]
-            totals[k] += jnp.where(sub == 0, below, jnp.where(sub == cells_y - 1, above, 0.0))
         return totals
 
     def half_sweep(colour, half, section):
@@ -355,13 +357,16 @@
             lanes = pl.ds(tile * LANES, LANES)
             totals = halo_terms(colour, half, p, tile)
             if section == 0:
-                results = [totals[k] * scale[colour, p, k, :, lanes] for k in range(states)]
+                results = [
+                    (part[p, k, :, lanes] + totals[k]) * scale[colour, p, k, :, lanes]
+                    for k in range(states)
+                ]
             else:
                 if tile == 0:
                     totals[0] += inflow[colour, p]
                 result = None
                 for t in range(states):
-                    driving = source[colour, p, t, :, lanes] + weights[t] * totals[t]
+                    driving = part[p, t, :, lanes] + weights[t] * totals[t]
                     term = matrix[colour, p, t, :, :, lanes] * driving
                     result = term if result is None else result + term
                 results = [result[k] for k in range(states)]

time: 31.7 us -> 31.3 us (0.987)
  Pallas kernels: 30.8 us -> 30.4 us
    pallas_call x1, Pallas kernels: 30.8 us -> 30.4 us  [shards(): pl.pallas_call(functools.partial(kernel, n_gx, n_gy, block), out_shape=ja...]
where the time goes in v6:
time: 31.3 us; the launch traced here: 31.2 us
  Pallas kernels  30.4 us (97%)
  local copies, waits for them, and re-layouts  0.77 us (2%)
    pallas_call x1, Pallas kernels, shards(): pl.pallas_call(functools.partial(kernel, n_gx, n_gy, block), out_shape=ja...  30.4 us
    unnamed x1, local copies, waits for them, and re-layouts  0.77 us

profile of v6, /device:TPU:3, one launch (start us, length us, event | category | flops | bytes accessed | tf_op | source)
XLA Modules:
  0.0 31.2 jit_solution(7640588966482051192)
XLA Ops:
  0.0 30.4 %shard_map.73 = f32[1,7,4,8,512]{4,3,2,1,0:T(8,128)S(1)} custom-call(f32[1,7,4,8,512]{4,3,2,1,0:T(8,128)} %fields.1, f32[1,7,4,8,512]{4,3,2,1,0:T(8,128)} %sources.1, f32[7,4,8,512]{3,2,1,0:T(8,128)} %diagonal.1, f32[7,7,4,8,512]{4,3,2,1,0:T(8,128)} %inverse.1, f32[7]{0:T(128)} %coupling.1, s32[3,16]{1,0:T(4,128)} %bitcast.1, s32[1,896]{1,0:T(1,128)} %returns.1), custom_call_target="tpu_custom_call" | custom-call | tf_op jit(solution)/shard_map/pallas_call | solution.py:438
  30.4 0.8 %copy.9 = f32[1,7,4,8,512]{4,3,2,1,0:T(8,128)} copy(f32[1,7,4,8,512]{4,3,2,1,0:T(8,128)S(1)} %shard_map.73) | data formatting | bytes 917504
